TPU v7x, 256 devices: a whole 4x4x8 slice. The times are simulated.
256 devices in a mesh: dp: 32 (over z_hi, x, core), tensor: 8 (over z_lo, y).
Axes of the slice: x: 4, y: 4, z: 8 (z_hi: 4, z_lo: 2; z = z_hi * 2 + z_lo), core: 2. Of those that a mesh axis runs over, the one named last changes fastest.
Arguments:
- resp_queries: bfloat16 [8192, 8192], P('dp', 'tensor'), may hold values from -80 to 80
- resp_keys: bfloat16 [8192, 1024], P('dp', 'tensor'), may hold values from -7 to 7
- resp_values: bfloat16 [8192, 1024], P('dp', 'tensor'), may hold values from -6 to 6
- prompt_keys: bfloat16 [4096, 4, 1024], P(('dp', 'tensor')), may hold values from -6 to 6
- prompt_values: bfloat16 [4096, 4, 1024], P(('dp', 'tensor')), may hold values from -6 to 6
- out_grad: bfloat16 [8192, 8192], P('dp', 'tensor'), may hold values from -6 to 6
- lengths: int32 [64], P('dp'), may hold values from 1 to 128, as said below
- prompt_of: int32 [32], replicated, may hold values from 0 to 3, as said below
Outputs:
- attn_out: bfloat16 [8192, 8192], P('dp', 'tensor')
- grad_queries: bfloat16 [8192, 8192], P('dp', 'tensor')
- grad_resp_keys: bfloat16 [8192, 1024], P('dp', 'tensor')
- grad_resp_values: bfloat16 [8192, 1024], P('dp', 'tensor')
- grad_prompt_keys: bfloat16 [4096, 4, 1024], P(('dp', 'tensor'))
- grad_prompt_values: bfloat16 [4096, 4, 1024], P(('dp', 'tensor'))
Inputs may be any that keep to these rules, and one draw needn't show every extreme that they name: `prompt_of`: each prompt index is named by exactly 8 entries. `lengths`: some response has all 128 tokens live in every draw.
All inputs are finite; a program needn't handle non-finite values.
Results may differ from a plain program's by a relative error of at most 0.007.
Values may be sent and summed in bfloat16 or wider, within the bound.
A program may use at most 64 MiB of HBM per device.

v0:
```python
import jax
import jax.numpy as jnp
from jax import lax
from jax.sharding import PartitionSpec as P

HEAD_DIM = 128


def head_pass(query_rows, prompt_k, prompt_v, own_k, own_v, grad_out, length):
    num_rows = query_rows.shape[0]
    prompt_span = prompt_k.shape[0]
    all_keys = jnp.concatenate([prompt_k, own_k], 0)
    all_values = jnp.concatenate([prompt_v, own_v], 0)
    scale_now = HEAD_DIM ** (-0.5)
    column_pos = (
        lax.broadcasted_iota(jnp.int32, (num_rows, prompt_span + num_rows), 1) - prompt_span
    )
    row_pos = lax.broadcasted_iota(jnp.int32, (num_rows, prompt_span + num_rows), 0)
    allowed = (column_pos < 0) | (column_pos <= row_pos) & (column_pos < length)
    valid_rows = lax.broadcasted_iota(jnp.int32, (num_rows, 1), 0) < length
    scores = jnp.dot(query_rows, all_keys.T, preferred_element_type=jnp.float32) * scale_now
    scores = jnp.where(allowed, scores, -1e30)
    row_max = jnp.max(scores, axis=1, keepdims=True)
    exp_terms = jnp.exp(scores - row_max)
    probs = exp_terms / jnp.sum(exp_terms, axis=1, keepdims=True)
    weights = probs.astype(jnp.bfloat16)
    mixed = jnp.dot(weights, all_values, preferred_element_type=jnp.float32)
    mixed = jnp.where(valid_rows, mixed, 0.0).astype(jnp.bfloat16)
    masked_grad = jnp.where(valid_rows, grad_out, jnp.zeros_like(grad_out))
    value_terms = jnp.dot(weights.T, masked_grad, preferred_element_type=jnp.float32)
    grad_w = jnp.dot(masked_grad, all_values.T, preferred_element_type=jnp.float32)
    row_inner = jnp.sum(grad_w * probs, axis=1, keepdims=True)
    dscore = (probs * (grad_w - row_inner) * scale_now).astype(jnp.bfloat16)
    grad_q = jnp.dot(dscore, all_keys, preferred_element_type=jnp.float32).astype(jnp.bfloat16)
    key_terms = jnp.dot(dscore.T, query_rows, preferred_element_type=jnp.float32)
    return (
        mixed,
        grad_q,
        key_terms[:prompt_span],
        value_terms[:prompt_span],
        key_terms[prompt_span:],
        value_terms[prompt_span:],
    )


def head_cols(source, index_now):
    start = index_now * HEAD_DIM
    return lax.dynamic_slice_in_dim(source, start, HEAD_DIM, 1)


def put_cols(target, piece, index_now):
    start = index_now * HEAD_DIM
    return lax.dynamic_update_slice_in_dim(target, piece, start, 1)


def device_pass(resp_queries, resp_keys, resp_values, span_k, span_v, out_grad, lengths):
    resp_count = lengths.shape[0]
    resp_len = resp_queries.shape[0] // resp_count
    q_count = resp_queries.shape[1] // HEAD_DIM
    kv_count = resp_keys.shape[1] // HEAD_DIM
    group_size = q_count // kv_count
    span_rows = span_k.shape[0]
    batched = jax.vmap(head_pass, in_axes=(0, None, None, 0, 0, 0, 0))

    def by_resp(source):
        return source.reshape(resp_count, resp_len, HEAD_DIM)

    def head_step(head_idx, state_now):
        mixed, grad_q, grad_pkeys, grad_pvalues, grad_rkeys, grad_rvalues = state_now
        head_idx = head_idx.astype(jnp.int32)
        kv_idx = head_idx // group_size
        results = batched(
            by_resp(head_cols(resp_queries, head_idx)),
            head_cols(span_k, kv_idx),
            head_cols(span_v, kv_idx),
            by_resp(head_cols(resp_keys, kv_idx)),
            by_resp(head_cols(resp_values, kv_idx)),
            by_resp(head_cols(out_grad, head_idx)),
            lengths,
        )
        mixed = put_cols(mixed, results[0].reshape(-1, HEAD_DIM), head_idx)
        grad_q = put_cols(grad_q, results[1].reshape(-1, HEAD_DIM), head_idx)
        grad_pkeys = put_cols(
            grad_pkeys, head_cols(grad_pkeys, kv_idx) + jnp.sum(results[2], 0), kv_idx
        )
        grad_pvalues = put_cols(
            grad_pvalues, head_cols(grad_pvalues, kv_idx) + jnp.sum(results[3], 0), kv_idx
        )
        grad_rkeys = put_cols(
            grad_rkeys, head_cols(grad_rkeys, kv_idx) + results[4].reshape(-1, HEAD_DIM), kv_idx
        )
        grad_rvalues = put_cols(
            grad_rvalues, head_cols(grad_rvalues, kv_idx) + results[5].reshape(-1, HEAD_DIM), kv_idx
        )
        return (mixed, grad_q, grad_pkeys, grad_pvalues, grad_rkeys, grad_rvalues)

    initial = (
        jnp.zeros(resp_queries.shape, jnp.bfloat16),
        jnp.zeros(resp_queries.shape, jnp.bfloat16),
        jnp.zeros((span_rows, resp_keys.shape[1]), jnp.float32),
        jnp.zeros((span_rows, resp_keys.shape[1]), jnp.float32),
        jnp.zeros(resp_keys.shape, jnp.float32),
        jnp.zeros(resp_keys.shape, jnp.float32),
    )
    return lax.fori_loop(0, q_count, head_step, initial)


def local(
    resp_queries, resp_keys, resp_values, prompt_keys, prompt_values, out_grad, lengths, prompt_of
):
    ranks = lax.axis_size("tensor")
    dp_count = lax.axis_size("dp")
    rows_here, prompt_count, full_width = prompt_keys.shape
    head_width = resp_keys.shape[1]
    block_rows = rows_here * ranks
    span_len = block_rows * dp_count
    block_k, block_v = (
        lax.all_to_all(
            prompt_keys.reshape(rows_here, prompt_count, ranks, head_width),
            "tensor",
            split_axis=2,
            concat_axis=0,
            tiled=True,
        ),
        lax.all_to_all(
            prompt_values.reshape(rows_here, prompt_count, ranks, head_width),
            "tensor",
            split_axis=2,
            concat_axis=0,
            tiled=True,
        ),
    )
    block_k = block_k.reshape(block_rows, prompt_count, head_width)
    block_v = block_v.reshape(block_rows, prompt_count, head_width)
    send_k = jnp.take(block_k, prompt_of, axis=1)
    send_v = jnp.take(block_v, prompt_of, axis=1)
    got_k, got_v = (
        lax.all_to_all(send_k, "dp", split_axis=1, concat_axis=0, tiled=True),
        lax.all_to_all(send_v, "dp", split_axis=1, concat_axis=0, tiled=True),
    )
    span_k = got_k.reshape(span_len, head_width)
    span_v = got_v.reshape(span_len, head_width)
    mixed, grad_q, grad_pkeys, grad_pvalues, grad_rkeys, grad_rvalues = device_pass(
        resp_queries, resp_keys, resp_values, span_k, span_v, out_grad, lengths
    )
    back_k, back_v = (
        lax.all_to_all(
            grad_pkeys.reshape(dp_count, block_rows, head_width),
            "dp",
            split_axis=0,
            concat_axis=0,
            tiled=True,
        ),
        lax.all_to_all(
            grad_pvalues.reshape(dp_count, block_rows, head_width),
            "dp",
            split_axis=0,
            concat_axis=0,
            tiled=True,
        ),
    )
    owners = (
        prompt_of[:, None] == lax.broadcasted_iota(jnp.int32, (dp_count, prompt_count), 1)
    ).astype(jnp.float32)
    summed_k = jnp.einsum("sp,srw->rpw", owners, back_k, precision=lax.Precision.HIGHEST)
    summed_v = jnp.einsum("sp,srw->rpw", owners, back_v, precision=lax.Precision.HIGHEST)
    rows_k, rows_v = (
        lax.all_to_all(
            summed_k.astype(jnp.bfloat16).reshape(ranks, rows_here, prompt_count, 1, head_width),
            "tensor",
            split_axis=0,
            concat_axis=3,
            tiled=True,
        ),
        lax.all_to_all(
            summed_v.astype(jnp.bfloat16).reshape(ranks, rows_here, prompt_count, 1, head_width),
            "tensor",
            split_axis=0,
            concat_axis=3,
            tiled=True,
        ),
    )
    return (
        mixed,
        grad_q,
        grad_rkeys.astype(jnp.bfloat16),
        grad_rvalues.astype(jnp.bfloat16),
        rows_k.reshape(rows_here, prompt_count, ranks * head_width),
        rows_v.reshape(rows_here, prompt_count, ranks * head_width),
    )


def solution(mesh):
    return jax.shard_map(
        local,
        mesh=mesh,
        in_specs=(
            P("dp", "tensor"),
            P("dp", "tensor"),
            P("dp", "tensor"),
            P(("dp", "tensor"), None, None),
            P(("dp", "tensor"), None, None),
            P("dp", "tensor"),
            P("dp"),
            P(),
        ),
        out_specs=(
            P("dp", "tensor"),
            P("dp", "tensor"),
            P("dp", "tensor"),
            P("dp", "tensor"),
            P(("dp", "tensor"), None, None),
            P(("dp", "tensor"), None, None),
        ),
        check_vma=False,
    )
```

profile of v0, /device:TPU:1, one launch (start us, length us, event | category | flops | bytes accessed | tf_op | source)
XLA Modules:
  0.0 388.3 jit_solution(9266179296786333367)
XLA Ops:
  2.3 6.4 %all-to-all-start.2 = ((bf16[16,4,8,128]{3,0,1,2:T(8,128)(2,1)}), bf16[16,4,8,128]{3,0,1,2:T(8,128)(2,1)S(1)}, u32[]{:S(2)}, u32[]{:S(2)}) async-start(bf16[16,4,8,128]{3,0,1,2:T(8,128)(2,1)} %copy.52), calls=%async_computation.2 | async-start | bytes 262144 | tf_op jit(solution)/shard_map/all_to_all | solution.py:125
  11.0 3.1 all-to-all-done.2
  14.1 3.4 all-to-all-start
  19.0 3.9 %all-to-all-done = bf16[16,4,8,128]{3,0,1,2:T(8,128)(2,1)S(1)} async-done(((bf16[16,4,8,128]{3,0,1,2:T(8,128)(2,1)}), bf16[16,4,8,128]{3,0,1,2:T(8,128)(2,1)S(1)}, u32[]{:S(2)}, u32[]{:S(2)}) %all-to-all-start) | async-done | bytes 131104 | tf_op jit(solution)/shard_map/all_to_all | solution.py:118
  24.9 42.0 %all_to_all.100 = bf16[128,32,128]{2,0,1:T(8,128)(2,1)S(1)} all-to-all(bf16[128,32,128]{2,0,1:T(8,128)(2,1)S(1)} %get-tuple-element.435), channel_id=1, replica_groups=mesh['dp'=32,'tensor'=8] {'dp'}, dimensions={1} | all-to-all | bytes 2097152 | tf_op jit(solution)/shard_map/all_to_all | solution.py:139
  66.9 5.8 %all-to-all-start.1 = ((bf16[128,32,128]{2,0,1:T(8,128)(2,1)}), bf16[128,32,128]{2,0,1:T(8,128)(2,1)}, u32[]{:S(2)}, u32[]{:S(2)}) async-start(bf16[128,32,128]{2,0,1:T(8,128)(2,1)} %get-tuple-element.436), calls=%async_computation.1 | async-start | bytes 2097152 | tf_op jit(solution)/shard_map/all_to_all | solution.py:138
  72.8 28.6 %all-to-all-done.1 = bf16[128,32,128]{2,0,1:T(8,128)(2,1)} async-done(((bf16[128,32,128]{2,0,1:T(8,128)(2,1)}), bf16[128,32,128]{2,0,1:T(8,128)(2,1)}, u32[]{:S(2)}, u32[]{:S(2)}) %all-to-all-start.1) | async-done | bytes 1048608 | tf_op jit(solution)/shard_map/all_to_all | solution.py:138
  103.1 153.8 %while.26 = (s32[]{:T(128)}, bf16[256,1024]{1,0:T(8,128)(2,1)}, bf16[256,1024]{1,0:T(8,128)(2,1)}, f32[4096,128]{1,0:T(8,128)S(1)}, f32[4096,128]{1,0:T(8,128)},...) while((s32[]{:T(128)}, bf16[256,1024]{1,0:T(8,128)(2,1)}, ...), condition=%wide.region_6.8_spmd.clone, body=%wide.region_0.7_spmd.clone.sunk | while | flops 1701713024 | bytes 110656552 | solution.py:105
  114.4 1.6 copy-done
  118.0 2.9 select_add_fusion.3
  132.2 1.6 copy-done
  135.8 4.5 %select_add_fusion.3 = (f32[4096,128]{1,0:T(8,128)}, f32[4096,128]{1,0:T(8,128)S(1)}) fusion(f32[4096,128]{1,0:T(8,128)S(1)} %slice_reduce_fusion.4, f32[4096,128]{1,0:T(8,128)} %get-tuple-element.560, pred[]{:T(512)S(6)} %compare.5, f32[4096,128]{1,0:T(8,128)S(1)} %slice_reduce_fusion.5, f32[4096,128]{1,0:T(8,128)S(1)} %get-tuple-element.559), kind=kLoop, calls=%fused_computation.23.clone.1 | loop fusion | flops 2097152 | bytes 12582913 | tf_op jit(solution)/shard_map/while/body/eval_jaxpr/add | solution.py:87
  151.6 1.6 copy-done
  155.2 4.5 %select_add_fusion.3 = (f32[4096,128]{1,0:T(8,128)}, f32[4096,128]{1,0:T(8,128)S(1)}) fusion(f32[4096,128]{1,0:T(8,128)S(1)} %slice_reduce_fusion.4, f32[4096,128]{1,0:T(8,128)} %get-tuple-element.560, pred[]{:T(512)S(6)} %compare.5, f32[4096,128]{1,0:T(8,128)S(1)} %slice_reduce_fusion.5, f32[4096,128]{1,0:T(8,128)S(1)} %get-tuple-element.559), kind=kLoop, calls=%fused_computation.23.clone.1 | loop fusion | flops 2097152 | bytes 12582913 | tf_op jit(solution)/shard_map/while/body/eval_jaxpr/add | solution.py:87
  171.0 1.6 copy-done
  174.6 4.5 %select_add_fusion.3 = (f32[4096,128]{1,0:T(8,128)}, f32[4096,128]{1,0:T(8,128)S(1)}) fusion(f32[4096,128]{1,0:T(8,128)S(1)} %slice_reduce_fusion.4, f32[4096,128]{1,0:T(8,128)} %get-tuple-element.560, pred[]{:T(512)S(6)} %compare.5, f32[4096,128]{1,0:T(8,128)S(1)} %slice_reduce_fusion.5, f32[4096,128]{1,0:T(8,128)S(1)} %get-tuple-element.559), kind=kLoop, calls=%fused_computation.23.clone.1 | loop fusion | flops 2097152 | bytes 12582913 | tf_op jit(solution)/shard_map/while/body/eval_jaxpr/add | solution.py:87
  190.4 1.6 copy-done
  194.0 4.5 %select_add_fusion.3 = (f32[4096,128]{1,0:T(8,128)}, f32[4096,128]{1,0:T(8,128)S(1)}) fusion(f32[4096,128]{1,0:T(8,128)S(1)} %slice_reduce_fusion.4, f32[4096,128]{1,0:T(8,128)} %get-tuple-element.560, pred[]{:T(512)S(6)} %compare.5, f32[4096,128]{1,0:T(8,128)S(1)} %slice_reduce_fusion.5, f32[4096,128]{1,0:T(8,128)S(1)} %get-tuple-element.559), kind=kLoop, calls=%fused_computation.23.clone.1 | loop fusion | flops 2097152 | bytes 12582913 | tf_op jit(solution)/shard_map/while/body/eval_jaxpr/add | solution.py:87
  209.8 1.6 copy-done
  213.5 4.5 %select_add_fusion.3 = (f32[4096,128]{1,0:T(8,128)}, f32[4096,128]{1,0:T(8,128)S(1)}) fusion(f32[4096,128]{1,0:T(8,128)S(1)} %slice_reduce_fusion.4, f32[4096,128]{1,0:T(8,128)} %get-tuple-element.560, pred[]{:T(512)S(6)} %compare.5, f32[4096,128]{1,0:T(8,128)S(1)} %slice_reduce_fusion.5, f32[4096,128]{1,0:T(8,128)S(1)} %get-tuple-element.559), kind=kLoop, calls=%fused_computation.23.clone.1 | loop fusion | flops 2097152 | bytes 12582913 | tf_op jit(solution)/shard_map/while/body/eval_jaxpr/add | solution.py:87
  229.3 1.6 copy-done
  232.9 4.5 %select_add_fusion.3 = (f32[4096,128]{1,0:T(8,128)}, f32[4096,128]{1,0:T(8,128)S(1)}) fusion(f32[4096,128]{1,0:T(8,128)S(1)} %slice_reduce_fusion.4, f32[4096,128]{1,0:T(8,128)} %get-tuple-element.560, pred[]{:T(512)S(6)} %compare.5, f32[4096,128]{1,0:T(8,128)S(1)} %slice_reduce_fusion.5, f32[4096,128]{1,0:T(8,128)S(1)} %get-tuple-element.559), kind=kLoop, calls=%fused_computation.23.clone.1 | loop fusion | flops 2097152 | bytes 12582913 | tf_op jit(solution)/shard_map/while/body/eval_jaxpr/add | solution.py:87
  252.3 4.5 %select_add_fusion.3 = (f32[4096,128]{1,0:T(8,128)}, f32[4096,128]{1,0:T(8,128)S(1)}) fusion(f32[4096,128]{1,0:T(8,128)S(1)} %slice_reduce_fusion.4, f32[4096,128]{1,0:T(8,128)} %get-tuple-element.560, pred[]{:T(512)S(6)} %compare.5, f32[4096,128]{1,0:T(8,128)S(1)} %slice_reduce_fusion.5, f32[4096,128]{1,0:T(8,128)S(1)} %get-tuple-element.559), kind=kLoop, calls=%fused_computation.23.clone.1 | loop fusion | flops 2097152 | bytes 12582913 | tf_op jit(solution)/shard_map/while/body/eval_jaxpr/add | solution.py:87
  256.9 56.5 %all_to_all.101 = f32[32,128,128]{2,1,0:T(8,128)} all-to-all(f32[32,128,128]{2,1,0:T(8,128)S(1)} %bitcast.93), channel_id=1, replica_groups=mesh['dp'=32,'tensor'=8] {'dp'}, dimensions={0} | all-to-all | bytes 4194304 | tf_op jit(solution)/shard_map/all_to_all | solution.py:147
  313.3 5.5 %all-to-all-start.6 = ((f32[32,128,128]{2,1,0:T(8,128)}), f32[32,128,128]{2,1,0:T(8,128)S(1)}, u32[]{:S(2)}, u32[]{:S(2)}) async-start(f32[32,128,128]{2,1,0:T(8,128)} %bitcast.21), calls=%async_computation.6 | async-start | bytes 4194304 | tf_op jit(solution)/shard_map/all_to_all | solution.py:154
  318.9 4.1 %fusion.31 = bf16[128,128,4]{1,2,0:T(4,128)(2,1)} fusion(f32[32,128,128]{2,1,0:T(8,128)} %all_to_all.101, s32[32]{0:T(128)S(1)} %copy-done.2), kind=kOutput, calls=%fused_computation.53 | convolution fusion | flops 25231488 | bytes 2228352 | tf_op jit(solution)/shard_map/sp,srw->rpw/dot_general | solution.py:165
  323.0 47.0 %all-to-all-done.6 = f32[32,128,128]{2,1,0:T(8,128)S(1)} async-done(((f32[32,128,128]{2,1,0:T(8,128)}), f32[32,128,128]{2,1,0:T(8,128)S(1)}, u32[]{:S(2)}, u32[]{:S(2)}) %all-to-all-start.6) | async-done | bytes 2097184 | tf_op jit(solution)/shard_map/all_to_all | solution.py:154
  369.9 3.4 all-to-all-start.5
  373.3 2.6 fusion.34
  375.9 2.8 all-to-all-done.5
  378.7 3.4 all-to-all-start.7
  384.2 3.3 all-to-all-done.7
  (225 shorter events, 119.0 us)
Async XLA Ops:
  2.3 11.8 %all-to-all-start.2 = ((bf16[16,4,8,128]{3,0,1,2:T(8,128)(2,1)}), bf16[16,4,8,128]{3,0,1,2:T(8,128)(2,1)S(1)}, u32[]{:S(2)}, u32[]{:S(2)}) async-start(bf16[16,4,8,128]{3,0,1,2:T(8,128)(2,1)} %copy.52), calls=%async_computation.2 | async-start | bytes 262144 | tf_op jit(solution)/shard_map/all_to_all | solution.py:125
  14.1 8.7 %all-to-all-start = ((bf16[16,4,8,128]{3,0,1,2:T(8,128)(2,1)}), bf16[16,4,8,128]{3,0,1,2:T(8,128)(2,1)S(1)}, u32[]{:S(2)}, u32[]{:S(2)}) async-start(bf16[16,4,8,128]{3,0,1,2:T(8,128)(2,1)} %copy.49), calls=%async_computation | async-start | bytes 262144 | tf_op jit(solution)/shard_map/all_to_all | solution.py:118
  24.9 78.2 %copy-start.1 = (bf16[256,128]{1,0:T(8,128)(2,1)S(1)}, bf16[256,128]{1,0:T(8,128)(2,1)}, u32[]{:S(2)}) copy-start(bf16[256,128]{1,0:T(8,128)(2,1)} %param.14) | copy-start | bytes 196612
  24.9 78.2 %copy-start.3 = (bf16[256,128]{1,0:T(8,128)(2,1)S(1)}, bf16[256,128]{1,0:T(8,128)(2,1)}, u32[]{:S(2)}) copy-start(bf16[256,128]{1,0:T(8,128)(2,1)} %param.13) | copy-start | bytes 196612
  24.9 78.2 %copy-start.4 = (s32[2]{0:T(128)S(1)}, s32[2]{0:T(128)}, u32[]{:S(2)}) copy-start(s32[2]{0:T(128)} %param.18) | copy-start | bytes 28
  66.9 34.5 %all-to-all-start.1 = ((bf16[128,32,128]{2,0,1:T(8,128)(2,1)}), bf16[128,32,128]{2,0,1:T(8,128)(2,1)}, u32[]{:S(2)}, u32[]{:S(2)}) async-start(bf16[128,32,128]{2,0,1:T(8,128)(2,1)} %get-tuple-element.436), calls=%async_computation.1 | async-start | bytes 2097152 | tf_op jit(solution)/shard_map/all_to_all | solution.py:138
  114.0 2.0 copy-start
  118.0 2.9 slice-start
  131.8 2.0 copy-start
  135.8 4.5 %slice-start = ((f32[2,4224,128]{2,1,0:T(8,128)}), f32[2,128,128]{2,1,0:T(8,128)S(1)}, s32[]{:S(2)}) async-start(f32[2,4224,128]{2,1,0:T(8,128)} %copy-done), calls=%async_computation.8 | async-start | bytes 262144 | tf_op jit(solution)/shard_map/while/body/eval_jaxpr/vmap()/slice | solution.py:42
  151.2 2.0 copy-start
  155.2 4.5 %slice-start = ((f32[2,4224,128]{2,1,0:T(8,128)}), f32[2,128,128]{2,1,0:T(8,128)S(1)}, s32[]{:S(2)}) async-start(f32[2,4224,128]{2,1,0:T(8,128)} %copy-done), calls=%async_computation.8 | async-start | bytes 262144 | tf_op jit(solution)/shard_map/while/body/eval_jaxpr/vmap()/slice | solution.py:42
  170.6 2.0 copy-start
  174.6 4.5 %slice-start = ((f32[2,4224,128]{2,1,0:T(8,128)}), f32[2,128,128]{2,1,0:T(8,128)S(1)}, s32[]{:S(2)}) async-start(f32[2,4224,128]{2,1,0:T(8,128)} %copy-done), calls=%async_computation.8 | async-start | bytes 262144 | tf_op jit(solution)/shard_map/while/body/eval_jaxpr/vmap()/slice | solution.py:42
  190.0 2.0 copy-start
  194.0 4.5 %slice-start = ((f32[2,4224,128]{2,1,0:T(8,128)}), f32[2,128,128]{2,1,0:T(8,128)S(1)}, s32[]{:S(2)}) async-start(f32[2,4224,128]{2,1,0:T(8,128)} %copy-done), calls=%async_computation.8 | async-start | bytes 262144 | tf_op jit(solution)/shard_map/while/body/eval_jaxpr/vmap()/slice | solution.py:42
  209.5 2.0 copy-start
  213.4 4.5 %slice-start = ((f32[2,4224,128]{2,1,0:T(8,128)}), f32[2,128,128]{2,1,0:T(8,128)S(1)}, s32[]{:S(2)}) async-start(f32[2,4224,128]{2,1,0:T(8,128)} %copy-done), calls=%async_computation.8 | async-start | bytes 262144 | tf_op jit(solution)/shard_map/while/body/eval_jaxpr/vmap()/slice | solution.py:42
  228.9 2.0 copy-start
  232.9 4.5 %slice-start = ((f32[2,4224,128]{2,1,0:T(8,128)}), f32[2,128,128]{2,1,0:T(8,128)S(1)}, s32[]{:S(2)}) async-start(f32[2,4224,128]{2,1,0:T(8,128)} %copy-done), calls=%async_computation.8 | async-start | bytes 262144 | tf_op jit(solution)/shard_map/while/body/eval_jaxpr/vmap()/slice | solution.py:42
  248.3 2.0 copy-start
  252.3 4.5 %slice-start = ((f32[2,4224,128]{2,1,0:T(8,128)}), f32[2,128,128]{2,1,0:T(8,128)S(1)}, s32[]{:S(2)}) async-start(f32[2,4224,128]{2,1,0:T(8,128)} %copy-done), calls=%async_computation.8 | async-start | bytes 262144 | tf_op jit(solution)/shard_map/while/body/eval_jaxpr/vmap()/slice | solution.py:42
  313.3 5.5 %copy-start.2 = (s32[32]{0:T(128)S(1)}, s32[32]{0:T(128)}, u32[]{:S(2)}) copy-start(s32[32]{0:T(128)} %param.19) | copy-start | bytes 388
  313.3 56.6 %all-to-all-start.6 = ((f32[32,128,128]{2,1,0:T(8,128)}), f32[32,128,128]{2,1,0:T(8,128)S(1)}, u32[]{:S(2)}, u32[]{:S(2)}) async-start(f32[32,128,128]{2,1,0:T(8,128)} %bitcast.21), calls=%async_computation.6 | async-start | bytes 4194304 | tf_op jit(solution)/shard_map/all_to_all | solution.py:154
  369.9 8.8 %all-to-all-start.5 = ((bf16[8,16,4,1,128]{4,2,1,3,0:T(4,128)(2,1)}), bf16[8,16,4,1,128]{4,2,1,3,0:T(4,128)(2,1)S(1)}, u32[]{:S(2)}, u32[]{:S(2)}) async-start(bf16[8,16,4,1,128]{4,2,1,3,0:T(4,128)(2,1)} %bitcast.18), calls=%async_computation.5 | async-start | bytes 262144 | tf_op jit(solution)/shard_map/all_to_all | solution.py:168
  378.7 8.7 %all-to-all-start.7 = ((bf16[8,16,4,1,128]{4,2,1,3,0:T(4,128)(2,1)}), bf16[8,16,4,1,128]{4,2,1,3,0:T(4,128)(2,1)S(1)}, u32[]{:S(2)}, u32[]{:S(2)}) async-start(bf16[8,16,4,1,128]{4,2,1,3,0:T(4,128)(2,1)} %bitcast.24), calls=%async_computation.7 | async-start | bytes 262144 | tf_op jit(solution)/shard_map/all_to_all | solution.py:175
where the time goes:
time: 391 us; the launch traced here: 388 us
  blocking collectives  98.5 us (25%)
  waiting for transfers between devices  88.8 us (23%)
  other arithmetic  67.1 us (17%)
  local copies, waits for them, and re-layouts  53.2 us (14%)
  matrix products  51.1 us (13%)
  starting transfers between devices  27.8 us (7%)
    all_to_all x1, blocking collectives, local(): lax.all_to_all(grad_pkeys.reshape(dp_count, block_rows, head_width), 'dp'...  56.5 us
    all_to_all x1, waiting for transfers between devices, local(): lax.all_to_all(grad_pvalues.reshape(dp_count, block_rows, head_width), 'd...  47 us
    all_to_all x1, blocking collectives, local(): lax.all_to_all(send_v, 'dp', split_axis=1, concat_axis=0, tiled=True)  42 us
    add x8, other arithmetic, head_step(): head_cols(grad_pvalues, kv_idx) + jnp.sum(results[3], 0)  34.4 us
    all_to_all x1, waiting for transfers between devices, local(): lax.all_to_all(send_k, 'dp', split_axis=1, concat_axis=0, tiled=True)  28.6 us
    dynamic_slice x16, local copies, waits for them, and re-layouts, head_cols(): return lax.dynamic_slice_in_dim(source, start, HEAD_DIM, 1)  13.6 us
    while x16, local copies, waits for them, and re-layouts  13 us
    broadcast_in_dim x8, local copies, waits for them, and re-layouts, head_pass(): all_keys = jnp.concatenate([prompt_k, own_k], 0)  12 us
  transfers between devices with their start and end apart: 6, of which 6 were waited for; matrix products, arithmetic and copies ran while one was open for 3% of the time, Pallas kernels for 0%

commit v1 on v0

v1 whole, which is shorter than its diff:
```python
import jax
import jax.numpy as jnp
from jax import lax
from jax.experimental import pallas as pl
from jax.experimental.pallas import tpu as pltpu
from jax.sharding import PartitionSpec as P

D = 128
F32 = jnp.float32
BF16 = jnp.bfloat16
SCALE = D ** -0.5
LOG2E = 1.4426950408889634
TKF, TRF, TKB, TRB = 2048, 256, 512, 1024


def dot_nt(a, b):
    return lax.dot_general(a, b, (((1,), (1,)), ((), ())), preferred_element_type=F32)


def dot_nn(a, b):
    return jnp.dot(a, b, preferred_element_type=F32)


def own_mask(len_ref, cols, resp_rows, dev_rows):
    key = lax.broadcasted_iota(jnp.int32, (dev_rows, cols), 0)
    row = lax.broadcasted_iota(jnp.int32, (dev_rows, cols), 1) % dev_rows
    length = jnp.where(key < resp_rows, len_ref[0], len_ref[1])
    return (key // resp_rows == row // resp_rows) & (key <= row) & (key % resp_rows < length)


def attn_kernel(q_ref, k_ref, v_ref, rk_ref, rv_ref, g_ref, len_ref,
                o_ref, dq_ref, drk_ref, drv_ref, dk_ref, dv_ref,
                qa, ga, m_s, l_s, d_s, ot, kt, vt, acc_k, acc_v):
    rows = q_ref.shape[0]
    heads = q_ref.shape[1] // D
    half = rows // 2
    span = k_ref.shape[0]
    row_ids = lax.broadcasted_iota(jnp.int32, (rows, D), 0)
    live = (row_ids % half) < jnp.where(row_ids < half, len_ref[0], len_ref[1])
    for h in range(heads):
        qa[pl.ds(h * rows, rows)] = q_ref[:, h * D:(h + 1) * D]
        g = g_ref[:, h * D:(h + 1) * D]
        ga[pl.ds(h * rows, rows)] = jnp.where(live, g, jnp.zeros_like(g))

    mask_f = own_mask(len_ref, TRF, half, rows)
    rvt = rv_ref[...].T

    def own_fwd(j, _):
        blk = pl.ds(j * TRF, TRF)
        s = jnp.where(mask_f, dot_nt(rk_ref[...], qa[blk]) * (SCALE * LOG2E), -1e30)
        m = jnp.max(s, axis=0, keepdims=True)
        e = jnp.exp2(s - m)
        m_s[:, blk] = m
        l_s[:, blk] = jnp.sum(e, axis=0, keepdims=True)
        ot[:, blk] = dot_nn(rvt, e.astype(BF16))
        return 0

    lax.fori_loop(0, heads * rows // TRF, own_fwd, 0)

    def fwd_chunk(i, _):
        ks = k_ref[pl.ds(i * TKF, TKF)]
        vt[...] = v_ref[pl.ds(i * TKF, TKF)].T
        kt[:, pl.ds(i * TKF, TKF)] = ks.T

        def fwd_rows(j, _):
            blk = pl.ds(j * TRF, TRF)
            s = dot_nt(k_ref[pl.ds(i * TKF, TKF)], qa[blk]) * (SCALE * LOG2E)
            m_old = m_s[:, blk]
            m = jnp.maximum(m_old, jnp.max(s, axis=0, keepdims=True))
            e = jnp.exp2(s - m)
            alpha = jnp.exp2(m_old - m)
            m_s[:, blk] = m
            l_s[:, blk] = l_s[:, blk] * alpha + jnp.sum(e, axis=0, keepdims=True)
            ot[:, blk] = ot[:, blk] * alpha + dot_nn(vt[...], e.astype(BF16))
            return 0

        lax.fori_loop(0, heads * rows // TRF, fwd_rows, 0)
        return 0

    lax.fori_loop(0, span // TKF, fwd_chunk, 0)

    for h in range(heads):
        blk = pl.ds(h * rows, rows)
        l = l_s[:, blk]
        o = ot[:, blk] / l
        d_s[:, blk] = jnp.sum(o * ga[blk].T.astype(F32), axis=0, keepdims=True)
        m_s[:, blk] = m_s[:, blk] + jnp.log2(l)
        o_ref[:, h * D:(h + 1) * D] = jnp.where(live, o.T, 0.0).astype(BF16)

    ot[...] = jnp.zeros_like(ot)
    mask_b = own_mask(len_ref, TRB, half, rows)
    rkt = rk_ref[...].T

    def bwd_block(ks, vs, kts, blk, mask):
        qb, gb = qa[blk], ga[blk]
        s = dot_nt(ks, qb) * (SCALE * LOG2E)
        p = jnp.exp2(s - m_s[:, blk])
        if mask is not None:
            p = jnp.where(mask, p, 0.0)
        dp = dot_nt(vs, gb)
        ds = (p * (dp - d_s[:, blk])).astype(BF16)
        dv = dot_nn(p.astype(BF16), gb)
        dk = dot_nn(ds, qb)
        ot[:, blk] += dot_nn(kts, ds)
        return dk, dv

    acc_k[...] = jnp.zeros_like(acc_k)
    acc_v[...] = jnp.zeros_like(acc_v)

    def own_bwd(j, _):
        dk, dv = bwd_block(rk_ref[...], rv_ref[...], rkt, pl.ds(j * TRB, TRB), mask_b)
        acc_k[:rows] += dk
        acc_v[:rows] += dv
        return 0

    lax.fori_loop(0, heads * rows // TRB, own_bwd, 0)
    drk_ref[...] = (acc_k[:rows] * SCALE).astype(BF16)
    drv_ref[...] = acc_v[:rows].astype(BF16)

    def bwd_chunk(i, _):
        cur = pl.ds(i * TKB, TKB)
        acc_k[...] = jnp.zeros_like(acc_k)
        acc_v[...] = jnp.zeros_like(acc_v)

        def bwd_rows(j, _):
            dk, dv = bwd_block(k_ref[cur], v_ref[cur], kt[:, cur], pl.ds(j * TRB, TRB), None)
            acc_k[...] += dk
            acc_v[...] += dv
            return 0

        lax.fori_loop(0, heads * rows // TRB, bwd_rows, 0)
        dk_ref[cur] = (acc_k[...] * SCALE).astype(BF16)
        dv_ref[cur] = acc_v[...].astype(BF16)
        return 0

    lax.fori_loop(0, span // TKB, bwd_chunk, 0)

    for h in range(heads):
        dq_ref[:, h * D:(h + 1) * D] = (ot[:, h * rows:(h + 1) * rows] * SCALE).T.astype(BF16)


def attention(q, k, v, rk, rv, g, lengths):
    rows, width = q.shape
    total = rows * width // D
    span = k.shape[0]
    vm = pl.BlockSpec(memory_space=pltpu.VMEM)
    return pl.pallas_call(
        attn_kernel,
        out_shape=(
            jax.ShapeDtypeStruct(q.shape, BF16),
            jax.ShapeDtypeStruct(q.shape, BF16),
            jax.ShapeDtypeStruct(rk.shape, BF16),
            jax.ShapeDtypeStruct(rk.shape, BF16),
            jax.ShapeDtypeStruct(k.shape, BF16),
            jax.ShapeDtypeStruct(k.shape, BF16),
        ),
        in_specs=[vm] * 6 + [pl.BlockSpec(memory_space=pltpu.SMEM)],
        out_specs=(vm,) * 6,
        scratch_shapes=[
            pltpu.VMEM((total, D), BF16), pltpu.VMEM((total, D), BF16),
            pltpu.VMEM((1, total), F32), pltpu.VMEM((1, total), F32), pltpu.VMEM((1, total), F32),
            pltpu.VMEM((D, total), F32), pltpu.VMEM((D, span), BF16), pltpu.VMEM((D, TKF), BF16),
            pltpu.VMEM((TKB, D), F32), pltpu.VMEM((TKB, D), F32),
        ],
        compiler_params=pltpu.CompilerParams(vmem_limit_bytes=56 * 2 ** 20),
        cost_estimate=pl.CostEstimate(flops=14 * total * span * D, bytes_accessed=6 * 2 ** 20, transcendentals=2 * total * span),
    )(q, k, v, rk, rv, g, lengths)


def local(
    resp_queries, resp_keys, resp_values, prompt_keys, prompt_values, out_grad, lengths, prompt_of
):
    ranks = lax.axis_size("tensor")
    dp_count = lax.axis_size("dp")
    rows_here, prompt_count, full_width = prompt_keys.shape
    head_width = resp_keys.shape[1]
    block_rows = rows_here * ranks
    span_len = block_rows * dp_count
    block_k, block_v = (
        lax.all_to_all(
            prompt_keys.reshape(rows_here, prompt_count, ranks, head_width),
            "tensor",
            split_axis=2,
            concat_axis=0,
            tiled=True,
        ),
        lax.all_to_all(
            prompt_values.reshape(rows_here, prompt_count, ranks, head_width),
            "tensor",
            split_axis=2,
            concat_axis=0,
            tiled=True,
        ),
    )
    block_k = block_k.reshape(block_rows, prompt_count, head_width)
    block_v = block_v.reshape(block_rows, prompt_count, head_width)
    send_k = jnp.take(block_k, prompt_of, axis=1)
    send_v = jnp.take(block_v, prompt_of, axis=1)
    got_k, got_v = (
        lax.all_to_all(send_k, "dp", split_axis=1, concat_axis=0, tiled=True),
        lax.all_to_all(send_v, "dp", split_axis=1, concat_axis=0, tiled=True),
    )
    span_k = got_k.reshape(span_len, head_width)
    span_v = got_v.reshape(span_len, head_width)
    mixed, grad_q, grad_rkeys, grad_rvalues, grad_pkeys, grad_pvalues = attention(
        resp_queries, span_k, span_v, resp_keys, resp_values, out_grad, lengths
    )
    back_k, back_v = (
        lax.all_to_all(
            grad_pkeys.reshape(dp_count, block_rows, head_width),
            "dp",
            split_axis=0,
            concat_axis=0,
            tiled=True,
        ),
        lax.all_to_all(
            grad_pvalues.reshape(dp_count, block_rows, head_width),
            "dp",
            split_axis=0,
            concat_axis=0,
            tiled=True,
        ),
    )
    owners = (
        prompt_of[:, None] == lax.broadcasted_iota(jnp.int32, (dp_count, prompt_count), 1)
    ).astype(BF16)
    summed_k = jnp.einsum("sp,srw->rpw", owners, back_k, preferred_element_type=F32)
    summed_v = jnp.einsum("sp,srw->rpw", owners, back_v, preferred_element_type=F32)
    rows_k, rows_v = (
        lax.all_to_all(
            summed_k.astype(jnp.bfloat16).reshape(ranks, rows_here, prompt_count, 1, head_width),
            "tensor",
            split_axis=0,
            concat_axis=3,
            tiled=True,
        ),
        lax.all_to_all(
            summed_v.astype(jnp.bfloat16).reshape(ranks, rows_here, prompt_count, 1, head_width),
            "tensor",
            split_axis=0,
            concat_axis=3,
            tiled=True,
        ),
    )
    return (
        mixed,
        grad_q,
        grad_rkeys,
        grad_rvalues,
        rows_k.reshape(rows_here, prompt_count, ranks * head_width),
        rows_v.reshape(rows_here, prompt_count, ranks * head_width),
    )


def solution(mesh):
    return jax.shard_map(
        local,
        mesh=mesh,
        in_specs=(
            P("dp", "tensor"),
            P("dp", "tensor"),
            P("dp", "tensor"),
            P(("dp", "tensor"), None, None),
            P(("dp", "tensor"), None, None),
            P("dp", "tensor"),
            P("dp"),
            P(),
        ),
        out_specs=(
            P("dp", "tensor"),
            P("dp", "tensor"),
            P("dp", "tensor"),
            P("dp", "tensor"),
            P(("dp", "tensor"), None, None),
            P(("dp", "tensor"), None, None),
        ),
        check_vma=False,
    )
```

time: 391 us -> 239 us (0.61)
  other arithmetic: 67.1 us -> 0.27 us
  Pallas kernels: 0 us -> 50.8 us
  matrix products: 51.1 us -> 2.65 us
  local copies, waits for them, and re-layouts: 53.2 us -> 5.53 us
  waiting for transfers between devices: 88.8 us -> 45.1 us
  blocking collectives: 98.5 us -> 110 us
  starting transfers between devices: 27.8 us -> 22 us
    pallas_call x0 -> x1, Pallas kernels: none -> 50.8 us  [attention(): pl.pallas_call(attn_kernel, out_shape=(jax.ShapeDtypeStruct(q.shape, BF16...]
    dot_general x50 -> x2, matrix products: 51.1 us -> 2.65 us  [the longest x1 1.33 us: local(): jnp.einsum('sp,srw->rpw', owners, back_k, preferred_element_type=F32)]
    add x16 -> x0, other arithmetic: 34.9 us -> none  [the longest x8 34.4 us: head_step(): head_cols(grad_pvalues, kv_idx) + jnp.sum(results[3], 0)]
    all_to_all x0 -> x1, blocking collectives: none -> 34.3 us  [local(): lax.all_to_all(send_k, 'dp', split_axis=1, concat_axis=0, tiled=True)]
    all_to_all x1 -> x0, waiting for transfers between devices: 28.6 us -> none  [local(): lax.all_to_all(send_k, 'dp', split_axis=1, concat_axis=0, tiled=True)]
    all_to_all x1, blocking collectives: 56.5 us -> 34.1 us  [local(): lax.all_to_all(grad_pkeys.reshape(dp_count, block_rows, head_width), 'dp'...]
    sub x24 -> x0, other arithmetic: 20.1 us -> none  [the longest x8 11.1 us: head_pass(): dscore = (probs * (grad_w - row_inner) * scale_now).astype(jnp.bfloat16)]
    all_to_all x1, waiting for transfers between devices: 47 us -> 27.3 us  [local(): lax.all_to_all(grad_pvalues.reshape(dp_count, block_rows, head_width), 'd...]
  transfers between devices with their start and end apart: 6 -> 5, of which waited for: 6 -> 5; matrix products, arithmetic and copies ran while one was open for 3% -> 2% of each run, Pallas kernels for 0% -> 0%
where the time goes in v1:
time: 239 us; the launch traced here: 237 us
  blocking collectives  110 us (46%)
  Pallas kernels  50.8 us (21%)
  waiting for transfers between devices  45.1 us (19%)
  starting transfers between devices  22 us (9%)
  local copies, waits for them, and re-layouts  5.53 us (2%)
  matrix products  2.65 us (1%)
    pallas_call x1, Pallas kernels, attention(): pl.pallas_call(attn_kernel, out_shape=(jax.ShapeDtypeStruct(q.shape, BF16...  50.8 us
    all_to_all x1, blocking collectives, local(): lax.all_to_all(send_v, 'dp', split_axis=1, concat_axis=0, tiled=True)  42 us
    all_to_all x1, blocking collectives, local(): lax.all_to_all(send_k, 'dp', split_axis=1, concat_axis=0, tiled=True)  34.3 us
    all_to_all x1, blocking collectives, local(): lax.all_to_all(grad_pkeys.reshape(dp_count, block_rows, head_width), 'dp'...  34.1 us
    all_to_all x1, waiting for transfers between devices, local(): lax.all_to_all(grad_pvalues.reshape(dp_count, block_rows, head_width), 'd...  27.3 us
    all_to_all x1, starting transfers between devices, local(): lax.all_to_all(prompt_values.reshape(rows_here, prompt_count, ranks, head...  6.51 us
    all_to_all x1, starting transfers between devices, local(): lax.all_to_all(grad_pvalues.reshape(dp_count, block_rows, head_width), 'd...  5.36 us
  transfers between devices with their start and end apart: 5, of which 5 were waited for; matrix products, arithmetic and copies ran while one was open for 2% of the time, Pallas kernels for 0%

profile of v1, /device:TPU:1, one launch (start us, length us, event | category | flops | bytes accessed | tf_op | source)
XLA Modules:
  0.0 237.5 jit_solution(10933924967881519349)
XLA Ops:
  0.6 1.0 reshape.96
  1.6 0.7 copy.44
  2.3 0.0 copy-start
  2.3 6.5 %all-to-all-start.2 = ((bf16[16,4,8,128]{3,0,1,2:T(8,128)(2,1)}), bf16[16,4,8,128]{3,0,1,2:T(8,128)(2,1)S(1)}, u32[]{:S(2)}, u32[]{:S(2)}) async-start(bf16[16,4,8,128]{3,0,1,2:T(8,128)(2,1)} %copy.44), calls=%async_computation.2 | async-start | bytes 262144 | tf_op jit(solution)/shard_map/all_to_all | solution.py:187
  8.8 0.0 copy-done
  8.8 0.1 reshape.95
  8.9 0.0 copy-start.1
  8.9 0.7 copy.41
  9.6 0.0 copy-done.1
  9.6 4.7 %all-to-all-done.2 = bf16[16,4,8,128]{3,0,1,2:T(8,128)(2,1)S(1)} async-done(((bf16[16,4,8,128]{3,0,1,2:T(8,128)(2,1)}), bf16[16,4,8,128]{3,0,1,2:T(8,128)(2,1)S(1)}, u32[]{:S(2)}, u32[]{:S(2)}) %all-to-all-start.2) | async-done | bytes 131104 | tf_op jit(solution)/shard_map/all_to_all | solution.py:187
  14.3 3.4 %all-to-all-start = ((bf16[16,4,8,128]{3,0,1,2:T(8,128)(2,1)}), bf16[16,4,8,128]{3,0,1,2:T(8,128)(2,1)S(1)}, u32[]{:S(2)}, u32[]{:S(2)}) async-start(bf16[16,4,8,128]{3,0,1,2:T(8,128)(2,1)} %copy.41), calls=%async_computation | async-start | bytes 262144 | tf_op jit(solution)/shard_map/all_to_all | solution.py:180
  17.7 0.7 gather_fusion.1
  18.4 4.6 %all-to-all-done = bf16[16,4,8,128]{3,0,1,2:T(8,128)(2,1)S(1)} async-done(((bf16[16,4,8,128]{3,0,1,2:T(8,128)(2,1)}), bf16[16,4,8,128]{3,0,1,2:T(8,128)(2,1)S(1)}, u32[]{:S(2)}, u32[]{:S(2)}) %all-to-all-start) | async-done | bytes 131104 | tf_op jit(solution)/shard_map/all_to_all | solution.py:180
  23.0 0.7 gather_fusion
  23.8 0.3 select_bitcast_fusion
  24.0 42.0 %all_to_all.100 = bf16[128,32,128]{2,0,1:T(8,128)(2,1)} all-to-all(bf16[128,32,128]{2,0,1:T(8,128)(2,1)S(1)} %get-tuple-element.25), channel_id=1, replica_groups=mesh['dp'=32,'tensor'=8] {'dp'}, dimensions={1} | all-to-all | bytes 2097152 | tf_op jit(solution)/shard_map/all_to_all | solution.py:201
  66.0 34.3 %all_to_all.101 = bf16[128,32,128]{2,0,1:T(8,128)(2,1)} all-to-all(bf16[128,32,128]{2,0,1:T(8,128)(2,1)S(1)} %get-tuple-element.26), channel_id=1, replica_groups=mesh['dp'=32,'tensor'=8] {'dp'}, dimensions={1} | all-to-all | bytes 2097152 | tf_op jit(solution)/shard_map/all_to_all | solution.py:200
  100.3 50.8 %shard_map.127 = (bf16[256,1024]{1,0:T(8,128)(2,1)}, bf16[256,1024]{1,0:T(8,128)(2,1)}, bf16[256,128]{1,0:T(8,128)(2,1)}, bf16[256,128]{1,0:T(8,128)(2,1)}, bf16...) custom-call(bf16[256,1024]{1,0:T(8,128)(2,1)} %q_ref.1, bf16[4096,128]{1,0:T(8,128)(2,1)} %bitcast.57, ...), custom_call_target="tpu_custom_call" | custom-call | flops 15032385536 | bytes 6291456 | tf_op jit(solution)/shard_map/pallas_call | solution.py:147
  151.1 34.1 %all_to_all.102 = bf16[32,128,128]{2,1,0:T(8,128)(2,1)S(1)} all-to-all(bf16[32,128,128]{2,1,0:T(8,128)(2,1)} %bitcast.58), channel_id=1, replica_groups=mesh['dp'=32,'tensor'=8] {'dp'}, dimensions={0} | all-to-all | bytes 2097152 | tf_op jit(solution)/shard_map/all_to_all | solution.py:209
  185.2 5.4 %all-to-all-start.6 = ((bf16[32,128,128]{2,1,0:T(8,128)(2,1)}), bf16[32,128,128]{2,1,0:T(8,128)(2,1)S(1)}, u32[]{:S(2)}, u32[]{:S(2)}) async-start(bf16[32,128,128]{2,1,0:T(8,128)(2,1)} %bitcast.21), calls=%async_computation.6 | async-start | bytes 2097152 | tf_op jit(solution)/shard_map/all_to_all | solution.py:216
  190.5 1.3 convolution_convert_fusion.1
  191.9 27.3 %all-to-all-done.6 = bf16[32,128,128]{2,1,0:T(8,128)(2,1)S(1)} async-done(((bf16[32,128,128]{2,1,0:T(8,128)(2,1)}), bf16[32,128,128]{2,1,0:T(8,128)(2,1)S(1)}, u32[]{:S(2)}, u32[]{:S(2)}) %all-to-all-start.6) | async-done | bytes 1048608 | tf_op jit(solution)/shard_map/all_to_all | solution.py:216
  219.2 3.4 %all-to-all-start.5 = ((bf16[8,16,4,1,128]{4,2,1,3,0:T(4,128)(2,1)}), bf16[8,16,4,1,128]{4,2,1,3,0:T(4,128)(2,1)S(1)}, u32[]{:S(2)}, u32[]{:S(2)}) async-start(bf16[8,16,4,1,128]{4,2,1,3,0:T(4,128)(2,1)} %bitcast.18), calls=%async_computation.5 | async-start | bytes 262144 | tf_op jit(solution)/shard_map/all_to_all | solution.py:230
  222.6 1.3 convolution_convert_fusion
  223.9 4.0 %all-to-all-done.5 = bf16[8,16,4,1,128]{4,2,1,3,0:T(4,128)(2,1)S(1)} async-done(((bf16[8,16,4,1,128]{4,2,1,3,0:T(4,128)(2,1)}), bf16[8,16,4,1,128]{4,2,1,3,0:T(4,128)(2,1)S(1)}, u32[]{:S(2)}, u32[]{:S(2)}) %all-to-all-start.5) | async-done | bytes 131104 | tf_op jit(solution)/shard_map/all_to_all | solution.py:230
  227.9 3.4 %all-to-all-start.7 = ((bf16[8,16,4,1,128]{4,2,1,3,0:T(4,128)(2,1)}), bf16[8,16,4,1,128]{4,2,1,3,0:T(4,128)(2,1)S(1)}, u32[]{:S(2)}, u32[]{:S(2)}) async-start(bf16[8,16,4,1,128]{4,2,1,3,0:T(4,128)(2,1)} %bitcast.24), calls=%async_computation.7 | async-start | bytes 262144 | tf_op jit(solution)/shard_map/all_to_all | solution.py:237
  231.3 0.1 copy.58
  231.4 0.7 reshape.97
  232.1 4.6 %all-to-all-done.7 = bf16[8,16,4,1,128]{4,2,1,3,0:T(4,128)(2,1)S(1)} async-done(((bf16[8,16,4,1,128]{4,2,1,3,0:T(4,128)(2,1)}), bf16[8,16,4,1,128]{4,2,1,3,0:T(4,128)(2,1)S(1)}, u32[]{:S(2)}, u32[]{:S(2)}) %all-to-all-start.7) | async-done | bytes 131104 | tf_op jit(solution)/shard_map/all_to_all | solution.py:237
  236.7 0.1 copy.59
  236.8 0.7 reshape.98
  (5 shorter events, 0.0 us)
Async XLA Ops:
  2.3 6.5 %copy-start = (bf16[16,4,1024]{2,1,0:T(4,128)(2,1)S(1)}, bf16[16,4,1024]{2,1,0:T(4,128)(2,1)}, u32[]{:S(2)}) copy-start(bf16[16,4,1024]{2,1,0:T(4,128)(2,1)} %param.13) | copy-start | bytes 393220
  2.3 12.0 %all-to-all-start.2 = ((bf16[16,4,8,128]{3,0,1,2:T(8,128)(2,1)}), bf16[16,4,8,128]{3,0,1,2:T(8,128)(2,1)S(1)}, u32[]{:S(2)}, u32[]{:S(2)}) async-start(bf16[16,4,8,128]{3,0,1,2:T(8,128)(2,1)} %copy.44), calls=%async_computation.2 | async-start | bytes 262144 | tf_op jit(solution)/shard_map/all_to_all | solution.py:187
  8.9 0.7 copy-start.1
  14.3 8.7 %all-to-all-start = ((bf16[16,4,8,128]{3,0,1,2:T(8,128)(2,1)}), bf16[16,4,8,128]{3,0,1,2:T(8,128)(2,1)S(1)}, u32[]{:S(2)}, u32[]{:S(2)}) async-start(bf16[16,4,8,128]{3,0,1,2:T(8,128)(2,1)} %copy.41), calls=%async_computation | async-start | bytes 262144 | tf_op jit(solution)/shard_map/all_to_all | solution.py:180
  185.2 34.0 %all-to-all-start.6 = ((bf16[32,128,128]{2,1,0:T(8,128)(2,1)}), bf16[32,128,128]{2,1,0:T(8,128)(2,1)S(1)}, u32[]{:S(2)}, u32[]{:S(2)}) async-start(bf16[32,128,128]{2,1,0:T(8,128)(2,1)} %bitcast.21), calls=%async_computation.6 | async-start | bytes 2097152 | tf_op jit(solution)/shard_map/all_to_all | solution.py:216
  219.2 8.7 %all-to-all-start.5 = ((bf16[8,16,4,1,128]{4,2,1,3,0:T(4,128)(2,1)}), bf16[8,16,4,1,128]{4,2,1,3,0:T(4,128)(2,1)S(1)}, u32[]{:S(2)}, u32[]{:S(2)}) async-start(bf16[8,16,4,1,128]{4,2,1,3,0:T(4,128)(2,1)} %bitcast.18), calls=%async_computation.5 | async-start | bytes 262144 | tf_op jit(solution)/shard_map/all_to_all | solution.py:230
  227.9 8.7 %all-to-all-start.7 = ((bf16[8,16,4,1,128]{4,2,1,3,0:T(4,128)(2,1)}), bf16[8,16,4,1,128]{4,2,1,3,0:T(4,128)(2,1)S(1)}, u32[]{:S(2)}, u32[]{:S(2)}) async-start(bf16[8,16,4,1,128]{4,2,1,3,0:T(4,128)(2,1)} %bitcast.24), calls=%async_computation.7 | async-start | bytes 262144 | tf_op jit(solution)/shard_map/all_to_all | solution.py:237

commit v2 on v1

v2 whole, which is shorter than its diff:
```python
import functools

import jax
import jax.numpy as jnp
from jax import lax
from jax.experimental import pallas as pl
from jax.experimental.pallas import tpu as pltpu
from jax.sharding import PartitionSpec as P

D = 128
F32 = jnp.float32
BF16 = jnp.bfloat16
SCALE = D ** -0.5
LOG2E = 1.4426950408889634
MESH = pl.DeviceIdType.MESH
PROMPTS = 4
RANKS = 8
Z, X, CORES = 4, 4, 2
PEERS = X * CORES
BLOCK = 128
CHUNK = PEERS * BLOCK
HALF = CHUNK // 2
TRF, TRB = 256, 512
X_ORDER = (2, 6, 3, 7, 4, 5, 1)


def dot_nt(a, b):
    return lax.dot_general(a, b, (((1,), (1,)), ((), ())), preferred_element_type=F32)


def dot_nn(a, b):
    return jnp.dot(a, b, preferred_element_type=F32)


def own_mask(len_ref, cols, resp_rows, dev_rows):
    key = lax.broadcasted_iota(jnp.int32, (dev_rows, cols), 0)
    row = lax.broadcasted_iota(jnp.int32, (dev_rows, cols), 1) % dev_rows
    length = jnp.where(key < resp_rows, len_ref[0], len_ref[1])
    return (key // resp_rows == row // resp_rows) & (key <= row) & (key % resp_rows < length)


def kernel(comm, owner_ref, len_ref, pin, q_ref, g_ref, rk_ref, rv_ref,
           o_ref, dq_ref, drk_ref, drv_ref, pout, *scratch):
    (zk, zv, xk, xv, ka, va, ts, t_own, qa, ga, m_s, mo_s, l_s, d_s, ot, vt, kt, acc_k, acc_v,
     gk, gv, rgk, rgv, sk, sv, rsk, rsv, sum_k, sum_v, bo_k, bo_v, back,
     t_send, t_recv, z_send, z_recv, x_send, x_recv,
     gx_send, gx_recv, gz_send, gz_recv, gt_send, gt_recv) = scratch
    rows = q_ref.shape[0]
    heads = q_ref.shape[1] // D
    half = rows // 2
    total = rows * heads

    dp, tensor = lax.axis_index("dp"), lax.axis_index("tensor")
    core, x_at, z_at = dp % CORES, dp // CORES % X, dp // (CORES * X)
    y_at, zl_at = tensor % 4, tensor // 4

    def dp_index(z, x, c):
        return (z * X + x) * CORES + c

    def x_peer(j, sign):
        return dp_index(z_at, (x_at + sign * (j // 2) + X) % X, (core + j) % CORES)

    def z_peer(d, sign):
        return dp_index((z_at + sign * d + Z) % Z, x_at, core)

    def t_peer(i):
        return (zl_at + i // 4) % 2 * 4 + (y_at + i) % 4

    def t_back(i):
        return (zl_at + i // 4) % 2 * 4 + (y_at - i % 4 + 4) % 4

    def remote(src, dst, send, recv, device):
        return pltpu.make_async_remote_copy(
            src_ref=src, dst_ref=dst, send_sem=send, recv_sem=recv, device_id=device, device_id_type=MESH)

    def rows_of(t):
        return pl.ds(pl.multiple_of(t * 16, 16), 16)

    owners = [owner_ref[x_peer(j, 1)] for j in range(PEERS)]

    def t_copy(i, kv):
        dst = (zk, zv)[kv][0]
        return remote(pin.at[t_peer(i), kv], dst.at[:, rows_of(tensor)],
                      t_send.at[2 * i + kv], t_recv.at[2 * i + kv], (dp, t_peer(i)))

    def z_copy(d, kv):
        ref = (zk, zv)[kv]
        return remote(ref[0], ref[d], z_send.at[2 * d + kv], z_recv.at[2 * d + kv], (z_peer(d, 1), tensor))

    def x_copy(d, kv, j):
        at = (d * 2 + kv) * PEERS + j
        return remote((xk, xv)[kv][d].at[j], (ka, va)[kv][d].at[pl.ds(j * BLOCK, BLOCK)],
                      x_send.at[at], x_recv.at[at], (x_peer(j, 1), tensor))

    def gx_copy(d, kv, j):
        at = (d * 2 + kv) * PEERS + j
        return remote((gk, gv)[kv][d].at[pl.ds(j * BLOCK, BLOCK)], (rgk, rgv)[kv][d].at[j],
                      gx_send.at[at], gx_recv.at[at], (x_peer(j, -1), tensor))

    def gz_copy(d, kv):
        return remote((sk, sv)[kv][d - 1], (rsk, rsv)[kv][d - 1],
                      gz_send.at[2 * d + kv], gz_recv.at[2 * d + kv], (z_peer(d, -1), tensor))

    def gt_copy(i, kv):
        return remote((bo_k, bo_v)[kv].at[:, rows_of(t_peer(i))], back.at[tensor, kv],
                      gt_send.at[2 * i + kv], gt_recv.at[2 * i + kv], (dp, t_peer(i)))

    def start(copies):
        if comm:
            for copy in copies:
                copy.start()

    def wait_recv(copies):
        if comm:
            for copy in copies:
                copy.wait_recv()

    def wait_send(copies):
        if comm:
            for copy in copies:
                copy.wait_send()

    if comm:
        barrier = pltpu.get_barrier_semaphore()
        for j in range(1, PEERS):
            pl.semaphore_signal(barrier, inc=1, device_id=(x_peer(j, -1), tensor), device_id_type=MESH)
        for d in range(1, Z):
            pl.semaphore_signal(barrier, inc=1, device_id=(z_peer(d, -1), tensor), device_id_type=MESH)
        for i in range(1, RANKS):
            pl.semaphore_signal(barrier, inc=1, device_id=(dp, t_back(i)), device_id_type=MESH)
        pl.semaphore_wait(barrier, PEERS - 1 + Z - 1 + RANKS - 1)

    t_all = [(i, kv) for kv in range(2) for i in range(1, RANKS)]
    start(t_copy(i, kv) for i, kv in t_all)
    for kv in range(2):
        (zk, zv)[kv][0][:, rows_of(tensor)] = pin[tensor, kv]

    row_ids = lax.broadcasted_iota(jnp.int32, (rows, D), 0)
    live = (row_ids % half) < jnp.where(row_ids < half, len_ref[0], len_ref[1])
    for h in range(heads):
        qa[h * rows:(h + 1) * rows] = q_ref[:, h * D:(h + 1) * D]
        g = g_ref[:, h * D:(h + 1) * D]
        ga[h * rows:(h + 1) * rows] = jnp.where(live, g, jnp.zeros_like(g))

    def select(d, kv):
        src, dst, own = (zk, zv)[kv][d], (xk, xv)[kv][d], (ka, va)[kv][d]
        own[0:BLOCK] = src[owners[0]]
        for j in X_ORDER:
            dst[j] = src[owners[j]]
            start([x_copy(d, kv, j)])

    def arrived(d, kv):
        wait_recv(x_copy(d, kv, j) for j in X_ORDER)

    def own_fwd():
        mask = own_mask(len_ref, TRF, half, rows)
        rvt = rv_ref[...].T

        def body(b, _):
            blk = pl.ds(pl.multiple_of(b * TRF, TRF), TRF)
            t = jnp.where(mask, dot_nt(rk_ref[...], qa[blk]) * (SCALE * LOG2E), -1e30)
            t_own[:, blk] = t
            m = jnp.max(t, axis=0, keepdims=True)
            e = jnp.exp2(t - m)
            m_s[:, blk] = m
            mo_s[:, blk] = m
            l_s[:, blk] = jnp.sum(e, axis=0, keepdims=True)
            ot[:, blk] = dot_nn(rvt, e.astype(BF16))
            return 0

        lax.fori_loop(0, total // TRF, body, 0)

    def score(d):
        def body(b, _):
            blk = pl.ds(pl.multiple_of(b * TRF, TRF), TRF)
            t = dot_nt(ka[d][...], qa[blk]) * (SCALE * LOG2E)
            ts[d][:, blk] = t
            m_s[:, blk] = jnp.maximum(m_s[:, blk], jnp.max(t, axis=0, keepdims=True))
            return 0

        lax.fori_loop(0, total // TRF, body, 0)

    def mix(d):
        vt[...] = va[d][...].T

        def body(b, _):
            blk = pl.ds(pl.multiple_of(b * TRF, TRF), TRF)
            m = m_s[:, blk]
            e = jnp.exp2(ts[d][:, blk] - m)
            alpha = jnp.exp2(mo_s[:, blk] - m)
            mo_s[:, blk] = m
            l_s[:, blk] = l_s[:, blk] * alpha + jnp.sum(e, axis=0, keepdims=True)
            ot[:, blk] = ot[:, blk] * alpha + dot_nn(vt[...], e.astype(BF16))
            return 0

        lax.fori_loop(0, total // TRF, body, 0)

    own_fwd()
    wait_recv(t_copy(i, 0) for i in range(1, RANKS))
    start([z_copy(1, 0), z_copy(3, 0)])
    select(0, 0)
    wait_recv(t_copy(i, 1) for i in range(1, RANKS))
    start([z_copy(1, 1), z_copy(3, 1)])
    select(0, 1)
    start([z_copy(2, 0), z_copy(2, 1)])
    arrived(0, 0)
    score(0)
    wait_recv([z_copy(1, 0)])
    select(1, 0)
    wait_recv([z_copy(3, 0)])
    select(3, 0)
    arrived(0, 1)
    mix(0)
    wait_recv([z_copy(1, 1)])
    select(1, 1)
    wait_recv([z_copy(3, 1)])
    select(3, 1)
    arrived(1, 0)
    score(1)
    arrived(3, 0)
    score(3)
    wait_recv([z_copy(2, 0)])
    select(2, 0)
    arrived(1, 1)
    mix(1)
    wait_recv([z_copy(2, 1)])
    select(2, 1)
    arrived(3, 1)
    mix(3)
    arrived(2, 0)
    score(2)
    arrived(2, 1)
    mix(2)

    for h in range(heads):
        blk = slice(h * rows, (h + 1) * rows)
        l = l_s[:, blk]
        o = ot[:, blk] / l
        d_s[:, blk] = jnp.sum(o * ga[blk].T.astype(F32), axis=0, keepdims=True)
        m_s[:, blk] = m_s[:, blk] + jnp.log2(l)
        o_ref[:, h * D:(h + 1) * D] = jnp.where(live, o.T, 0.0).astype(BF16)
    ot[...] = jnp.zeros_like(ot)

    def bwd_block(t, vs, kts, blk):
        qb, gb = qa[blk], ga[blk]
        p = jnp.exp2(t - m_s[:, blk])
        ds = (p * (dot_nt(vs, gb) - d_s[:, blk])).astype(BF16)
        dv = dot_nn(p.astype(BF16), gb)
        dk = dot_nn(ds, qb)
        ot[:, blk] += dot_nn(kts, ds)
        return dk, dv

    def bwd_half(d, part):
        at = slice(part * HALF, (part + 1) * HALF)
        kt[...] = ka[d][at].T
        acc_k[...] = jnp.zeros_like(acc_k)
        acc_v[...] = jnp.zeros_like(acc_v)

        def body(b, _):
            blk = pl.ds(pl.multiple_of(b * TRB, TRB), TRB)
            dk, dv = bwd_block(ts[d][at, blk], va[d][at], kt[...], blk)
            acc_k[...] += dk
            acc_v[...] += dv
            return 0

        lax.fori_loop(0, total // TRB, body, 0)
        gk[d][at] = (acc_k[...] * SCALE).astype(BF16)
        gv[d][at] = acc_v[...].astype(BF16)
        start(gx_copy(d, kv, j) for j in X_ORDER if j // (PEERS // 2) == part for kv in range(2))

    def own_bwd():
        rkt = rk_ref[...].T
        acc_k[:rows] = jnp.zeros((rows, D), F32)
        acc_v[:rows] = jnp.zeros((rows, D), F32)

        def body(b, _):
            blk = pl.ds(pl.multiple_of(b * TRB, TRB), TRB)
            dk, dv = bwd_block(t_own[:, blk], rv_ref[...], rkt, blk)
            acc_k[:rows] += dk
            acc_v[:rows] += dv
            return 0

        lax.fori_loop(0, total // TRB, body, 0)
        drk_ref[...] = (acc_k[:rows] * SCALE).astype(BF16)
        drv_ref[...] = acc_v[:rows].astype(BF16)

    picks = [[(owners[j] == p).astype(F32) for j in range(PEERS)] for p in range(PROMPTS)]

    def by_prompt(d, kv, at):
        mine, got = (gk, gv)[kv][d], (rgk, rgv)[kv][d]
        terms = [mine[at].astype(F32)] + [got[j, at].astype(F32) for j in range(1, PEERS)]
        sums = []
        for p in range(PROMPTS):
            value = terms[0] * picks[p][0]
            for j in range(1, PEERS):
                value = value + terms[j] * picks[p][j]
            sums.append(value)
        return sums

    def reduce(d):
        for kv in range(2):
            wait_recv(gx_copy(d, kv, j) for j in X_ORDER)

            def body(b, _):
                at = rows_of(b)
                for p, value in enumerate(by_prompt(d, kv, at)):
                    (sk, sv)[kv][d - 1][p, at] = value.astype(BF16)
                return 0

            lax.fori_loop(0, BLOCK // 16, body, 0)
            start([gz_copy(d, kv)])

    def reduce_own(kv):
        wait_recv(gx_copy(0, kv, j) for j in X_ORDER)

        def body(b, _):
            at = rows_of(b)
            for p, value in enumerate(by_prompt(0, kv, at)):
                (sum_k, sum_v)[kv][p, at] = value
            return 0

        lax.fori_loop(0, BLOCK // 16, body, 0)

    def gather_sums(kv):
        wait_recv(gz_copy(d, kv) for d in (2, 1, 3))
        got = (rsk, rsv)[kv]

        def body(b, _):
            at = rows_of(b)
            for p in range(PROMPTS):
                value = (sum_k, sum_v)[kv][p, at]
                for d in range(Z - 1):
                    value = value + got[d][p, at].astype(F32)
                (bo_k, bo_v)[kv][p, at] = value.astype(BF16)
            return 0

        lax.fori_loop(0, BLOCK // 16, body, 0)
        start(gt_copy(i, kv) for i in range(1, RANKS))
        back[tensor, kv] = (bo_k, bo_v)[kv][:, rows_of(tensor)]

    bwd_half(2, 0)
    bwd_half(2, 1)
    bwd_half(1, 0)
    reduce(2)
    bwd_half(1, 1)
    bwd_half(3, 0)
    reduce(1)
    bwd_half(3, 1)
    bwd_half(0, 0)
    reduce(3)
    bwd_half(0, 1)
    own_bwd()
    for h in range(heads):
        dq_ref[:, h * D:(h + 1) * D] = (ot[:, h * rows:(h + 1) * rows] * SCALE).T.astype(BF16)
    reduce_own(0)
    reduce_own(1)
    gather_sums(0)
    gather_sums(1)
    wait_recv(gt_copy(i, kv) for i, kv in t_all)
    pout[...] = back[...]

    wait_send(t_copy(i, kv) for i, kv in t_all)
    wait_send(z_copy(d, kv) for d in range(1, Z) for kv in range(2))
    wait_send(x_copy(d, kv, j) for d in range(Z) for kv in range(2) for j in X_ORDER)
    wait_send(gx_copy(d, kv, j) for d in range(Z) for kv in range(2) for j in X_ORDER)
    wait_send(gz_copy(d, kv) for d in range(1, Z) for kv in range(2))
    wait_send(gt_copy(i, kv) for i, kv in t_all)


def attention(owner, lengths, pin, q, g, rk, rv, comm=True):
    rows, width = q.shape
    total = rows * width // D
    vm = pl.BlockSpec(memory_space=pltpu.VMEM)
    sm = pl.BlockSpec(memory_space=pltpu.SMEM)
    vmem = pltpu.VMEM
    dma = pltpu.SemaphoreType.DMA

    def some(count, shape, dtype=BF16):
        return [vmem(shape, dtype) for _ in range(count)]

    prompts = (PROMPTS, BLOCK, D)
    scratch = [
        some(Z, prompts), some(Z, prompts),
        some(Z, (PEERS, BLOCK, D)), some(Z, (PEERS, BLOCK, D)),
        some(Z, (CHUNK, D)), some(Z, (CHUNK, D)),
        some(Z, (CHUNK, total), F32), vmem((rows, total), F32),
        vmem((total, D), BF16), vmem((total, D), BF16),
        vmem((1, total), F32), vmem((1, total), F32), vmem((1, total), F32), vmem((1, total), F32),
        vmem((D, total), F32), vmem((D, CHUNK), BF16), vmem((D, HALF), BF16),
        vmem((HALF, D), F32), vmem((HALF, D), F32),
        some(Z, (CHUNK, D)), some(Z, (CHUNK, D)),
        some(Z, (PEERS, BLOCK, D)), some(Z, (PEERS, BLOCK, D)),
        some(Z - 1, prompts), some(Z - 1, prompts), some(Z - 1, prompts), some(Z - 1, prompts),
        vmem(prompts, F32), vmem(prompts, F32), vmem(prompts, BF16), vmem(prompts, BF16),
        vmem((RANKS, 2, PROMPTS, 16, D), BF16),
        dma((2 * RANKS,)), dma((2 * RANKS,)), dma((2 * Z,)), dma((2 * Z,)),
        dma((2 * Z * PEERS,)), dma((2 * Z * PEERS,)), dma((2 * Z * PEERS,)), dma((2 * Z * PEERS,)),
        dma((2 * Z,)), dma((2 * Z,)), dma((2 * RANKS,)), dma((2 * RANKS,)),
    ]
    extra = dict(collective_id=0, has_side_effects=True) if comm else {}
    return pl.pallas_call(
        functools.partial(kernel, comm),
        out_shape=(
            jax.ShapeDtypeStruct(q.shape, BF16),
            jax.ShapeDtypeStruct(q.shape, BF16),
            jax.ShapeDtypeStruct(rk.shape, BF16),
            jax.ShapeDtypeStruct(rk.shape, BF16),
            jax.ShapeDtypeStruct(pin.shape, BF16),
        ),
        in_specs=[sm, sm] + [vm] * 5,
        out_specs=(vm,) * 5,
        scratch_shapes=scratch,
        compiler_params=pltpu.CompilerParams(vmem_limit_bytes=62 * 2 ** 20, **extra),
    )(owner, lengths, pin, q, g, rk, rv)


def local(q, rk, rv, prompt_keys, prompt_values, g, lengths, prompt_of):
    rows_here, prompts, width = prompt_keys.shape
    both = jnp.stack([prompt_keys, prompt_values]).reshape(2, rows_here, prompts, RANKS, D)
    pin = jnp.transpose(both, (3, 0, 2, 1, 4))
    o, dq, drk, drv, back = attention(prompt_of, lengths, pin, q, g, rk, rv)
    back = jnp.transpose(back, (1, 3, 2, 0, 4)).reshape(2, rows_here, prompts, width)
    return o, dq, drk, drv, back[0], back[1]


def solution(mesh):
    heads = P("dp", "tensor")
    prompt = P(("dp", "tensor"), None, None)
    return jax.shard_map(
        local,
        mesh=mesh,
        in_specs=(heads, heads, heads, prompt, prompt, heads, P("dp"), P()),
        out_specs=(heads, heads, heads, heads, prompt, prompt),
        check_vma=False,
    )
```

time: 239 us -> 120 us (0.50)
  blocking collectives: 110 us -> 0 us
  Pallas kernels: 50.8 us -> 110 us
  waiting for transfers between devices: 45.1 us -> 0 us
  starting transfers between devices: 22 us -> 0 us
  matrix products: 2.65 us -> 0 us
  local copies, waits for them, and re-layouts: 5.53 us -> 8.11 us
    all_to_all x3 -> x0, blocking collectives: 110 us -> none  [the longest x1 42 us: local(): lax.all_to_all(send_v, 'dp', split_axis=1, concat_axis=0, tiled=True)]
    pallas_call x1, Pallas kernels: 50.8 us -> 110 us  [attention(): pl.pallas_call(functools.partial(kernel, comm), out_shape=(jax.ShapeDtype...]
    all_to_all x5 -> x0, waiting for transfers between devices: 45.1 us -> none  [the longest x1 27.3 us: local(): lax.all_to_all(grad_pvalues.reshape(dp_count, block_rows, head_width), 'd...]
    all_to_all x5 -> x0, starting transfers between devices: 22 us -> none  [the longest x1 6.51 us: local(): lax.all_to_all(prompt_values.reshape(rows_here, prompt_count, ranks, head...]
    unnamed x8 -> x18, local copies, waits for them, and re-layouts: 1.57 us -> 5.99 us
    dot_general x2 -> x0, matrix products: 2.65 us -> none  [the longest x1 1.33 us: local(): jnp.einsum('sp,srw->rpw', owners, back_k, preferred_element_type=F32)]
    reshape x4 -> x0, local copies, waits for them, and re-layouts: 2.44 us -> none  [the longest x2 1.67 us: local(): prompt_values.reshape(rows_here, prompt_count, ranks, head_width)]
  transfers between devices with their start and end apart: 5 -> 0, of which waited for: 5 -> 0; matrix products, arithmetic and copies ran while one was open for 2% -> 0% of each run, Pallas kernels for 0% -> 0%
where the time goes in v2:
time: 120 us; the launch traced here: 119 us
  Pallas kernels  110 us (92%)
  local copies, waits for them, and re-layouts  8.11 us (7%)
    pallas_call x1, Pallas kernels, attention(): pl.pallas_call(functools.partial(kernel, comm), out_shape=(jax.ShapeDtype...  110 us
    unnamed x18, local copies, waits for them, and re-layouts  5.99 us

profile of v2, /device:TPU:1, one launch (start us, length us, event | category | flops | bytes accessed | tf_op | source)
XLA Modules:
  0.0 119.4 jit_solution(15648183282704197990)
XLA Ops:
  0.6 1.0 reshape.22
  1.6 0.0 copy-start.2
  1.6 0.1 copy.16
  1.7 0.8 copy-done.2
  2.5 0.1 reshape.23
  2.6 0.1 copy.17
  2.6 0.7 maximum_bitcast_fusion.pin
  3.4 109.9 %shard_map.127 = (bf16[256,1024]{1,0:T(8,128)(2,1)}, bf16[256,1024]{1,0:T(8,128)(2,1)}, bf16[256,128]{1,0:T(8,128)(2,1)}, bf16[256,128]{1,0:T(8,128)(2,1)}, bf16[8,2,4,16,128]{4,3,2,1,0:T(8,128)(2,1)}) custom-call(s32[32]{0:T(128)} %owner_ref.1, s32[2]{0:T(128)} %len_ref.1, bf16[8,2,4,16,128]{4,3,2,1,0:T(8,128)(2,1)} %maximum_bitcast_fusion.pin, ...), custom_call_target="tpu_custom_call" | custom-call | tf_op jit(solution)/shard_map/pallas_call | solution.py:401
  113.2 1.0 fusion
  114.2 0.0 copy-start.1
  114.2 0.1 copy.27
  114.3 0.7 reshape.25
  115.0 0.1 copy.26
  115.1 0.7 reshape.24
  115.8 0.0 copy-done.1
  115.8 0.0 copy-start
  115.8 0.8 copy.34
  116.6 0.4 copy-done
  117.0 0.0 copy-start.4
  117.0 0.8 copy.35
  117.8 0.1 copy-done.4
  117.9 0.0 copy-start.3
  117.9 0.6 copy.36
  118.5 0.2 copy-done.3
  118.8 0.6 copy.37
Async XLA Ops:
  1.6 0.9 copy-start.2
  114.2 1.6 %copy-start.1 = (bf16[256,1024]{1,0:T(8,128)(2,1)S(1)}, bf16[256,1024]{1,0:T(8,128)(2,1)}, u32[]{:S(2)}) copy-start(bf16[256,1024]{1,0:T(8,128)(2,1)} %get-tuple-element.30) | copy-start | bytes 1572868
  115.8 1.2 %copy-start = (bf16[256,1024]{1,0:T(8,128)(2,1)S(1)}, bf16[256,1024]{1,0:T(8,128)(2,1)}, u32[]{:S(2)}) copy-start(bf16[256,1024]{1,0:T(8,128)(2,1)} %get-tuple-element.31) | copy-start | bytes 1572868
  117.0 0.9 copy-start.4
  117.9 0.9 copy-start.3

commit v3 on v2

v3 whole, which is shorter than its diff:
```python
import functools

import jax
import jax.numpy as jnp
from jax import lax
from jax.experimental import pallas as pl
from jax.experimental.pallas import tpu as pltpu
from jax.sharding import PartitionSpec as P

D = 128
F32 = jnp.float32
BF16 = jnp.bfloat16
SCALE = D ** -0.5
LOG2E = 1.4426950408889634
MESH = pl.DeviceIdType.MESH
PROMPTS = 4
RANKS = 8
Z, X, CORES = 4, 4, 2
PEERS = X * CORES
PARTS = 2
BLOCK = 64
UNIT = PEERS * BLOCK
TRF, TRB = 1024, 1024
X_ORDER = (2, 6, 3, 7, 4, 5, 1)


def dot_nt(a, b):
    return lax.dot_general(a, b, (((1,), (1,)), ((), ())), preferred_element_type=F32)


def dot_nn(a, b):
    return jnp.dot(a, b, preferred_element_type=F32)


def own_mask(len_ref, cols, resp_rows, dev_rows):
    key = lax.broadcasted_iota(jnp.int32, (dev_rows, cols), 0)
    row = lax.broadcasted_iota(jnp.int32, (dev_rows, cols), 1) % dev_rows
    length = jnp.where(key < resp_rows, len_ref[0], len_ref[1])
    return (key // resp_rows == row // resp_rows) & (key <= row) & (key % resp_rows < length)


def kernel(comm, owner_ref, len_ref, pk_hbm, pv_hbm, q_hbm, g_hbm, rk_hbm, rv_hbm,
           o_hbm, dq_hbm, drk_hbm, drv_hbm, pko_hbm, pvo_hbm, *scratch):
    (pk, pv, q_in, g_in, rk, rv, o_out, dq_out, drk, drv, pin, back,
     own_zk, own_zv, zk, zv, xk, xv, ka, va, ts, t_own, qa, ga, gat, m_s, mo_s, l_s, d_s, ot, dqt, vt, kt,
     acc_k, acc_v, gu, rgu, su, rsu, relay, own_sum, bo,
     io, t_send, t_recv, z_send, z_recv, x_send, x_recv,
     gx_send, gx_recv, gz_send, gz_recv, gt_send, gt_recv) = scratch
    rows, width = q_in.shape
    heads = width // D
    half = rows // 2
    total = rows * heads

    dp, tensor = lax.axis_index("dp"), lax.axis_index("tensor")
    core, x_at, z_at = dp % CORES, dp // CORES % X, dp // (CORES * X)
    y_at, zl_at = tensor % 4, tensor // 4

    def dp_index(z, x, c):
        return (z * X + x) * CORES + c

    def x_peer(j, sign):
        return dp_index(z_at, (x_at + sign * (j // 2) + X) % X, (core + j) % CORES)

    def z_peer(step):
        return dp_index((z_at + step + Z) % Z, x_at, core)

    def t_peer(i):
        return (zl_at + i // 4) % 2 * 4 + (y_at + i) % 4

    def t_back(i):
        return (zl_at + i // 4) % 2 * 4 + (y_at - i % 4 + 4) % 4

    def remote(src, dst, send, recv, device):
        return pltpu.make_async_remote_copy(
            src_ref=src, dst_ref=dst, send_sem=send, recv_sem=recv, device_id=device, device_id_type=MESH)

    def rows_of(t):
        return pl.ds(pl.multiple_of(t * 16, 16), 16)

    owners = [owner_ref[x_peer(j, 1)] for j in range(PEERS)]

    def t_copy(i, kv):
        dst = (own_zk, own_zv)[kv]
        return remote(pin.at[t_peer(i), kv], dst.at[tensor // 4, :, rows_of(tensor % 4)],
                      t_send.at[2 * i + kv], t_recv.at[2 * i + kv], (dp, t_peer(i)))

    def z_block(d, r, kv):
        return (own_zk, own_zv)[kv].at[r] if d == 0 else (zk, zv)[kv][2 * d + r]

    def z_copy(d, r, kv):
        at = (d * 2 + r) * 2 + kv
        src = z_block(0, r, kv) if d != 2 else z_block((1, 3)[r], r, kv)
        step = {1: 1, 3: -1, 2: (1, -1)[r]}[d]
        return remote(src, z_block(d, r, kv), z_send.at[at], z_recv.at[at], (z_peer(step), tensor))

    def x_copy(d, r, kv, j):
        u = 2 * d + r
        at = (u * 2 + kv) * PEERS + j
        return remote((xk, xv)[kv][u].at[j], (ka, va)[kv][u].at[pl.ds(j * BLOCK, BLOCK)],
                      x_send.at[at], x_recv.at[at], (x_peer(j, 1), tensor))

    def gx_copy(d, r, j):
        u = 2 * d + r
        at = u * PEERS + j
        return remote(gu[u].at[j], rgu[u].at[j], gx_send.at[at], gx_recv.at[at], (x_peer(j, -1), tensor))

    def gz_copy(d, r):
        u = 2 * d + r
        dst = relay[r] if d == 2 else rsu[u]
        step = {1: -1, 3: 1, 2: (-1, 1)[r]}[d]
        return remote(su[u], dst, gz_send.at[u], gz_recv.at[u], (z_peer(step), tensor))

    def gt_copy(i):
        to = t_peer(i)
        return remote(bo.at[to // 4, :, :, rows_of(to % 4)], back.at[tensor],
                      gt_send.at[i], gt_recv.at[i], (dp, to))

    def start(copies):
        if comm:
            for copy in copies:
                copy.start()

    def wait_recv(copies):
        if comm:
            for copy in copies:
                copy.wait_recv()

    def wait_send(copies):
        if comm:
            for copy in copies:
                copy.wait_send()

    loads = [pltpu.make_async_copy(src, dst, io.at[n]) for n, (src, dst) in enumerate(
        [(pk_hbm, pk), (pv_hbm, pv), (q_hbm, q_in), (g_hbm, g_in), (rk_hbm, rk), (rv_hbm, rv)])]
    stores = [pltpu.make_async_copy(src, dst, io.at[6 + n]) for n, (src, dst) in enumerate(
        [(o_out, o_hbm), (dq_out, dq_hbm), (drk, drk_hbm), (drv, drv_hbm), (pk, pko_hbm), (pv, pvo_hbm)])]
    for copy in loads:
        copy.start()

    if comm:
        barrier = pltpu.get_barrier_semaphore()
        for j in range(1, PEERS):
            pl.semaphore_signal(barrier, inc=1, device_id=(x_peer(j, -1), tensor), device_id_type=MESH)
        for step in (1, -1):
            pl.semaphore_signal(barrier, inc=1, device_id=(z_peer(step), tensor), device_id_type=MESH)
        for i in range(1, RANKS):
            pl.semaphore_signal(barrier, inc=1, device_id=(dp, t_back(i)), device_id_type=MESH)

    for kv in range(2):
        loads[kv].wait()
        for t in range(RANKS):
            for p in range(PROMPTS):
                at = p * RANKS * D + t * D
                pin[t, kv, p] = (pk, pv)[kv][:, at:at + D]
    if comm:
        pl.semaphore_wait(barrier, PEERS - 1 + 2 + RANKS - 1)

    t_all = [(i, kv) for kv in range(2) for i in range(1, RANKS)]
    start(t_copy(i, kv) for i, kv in t_all)
    for kv in range(2):
        (own_zk, own_zv)[kv][tensor // 4, :, rows_of(tensor % 4)] = pin[tensor, kv]
    for copy in loads[2:]:
        copy.wait()

    row_ids = lax.broadcasted_iota(jnp.int32, (rows, D), 0)
    live = (row_ids % half) < jnp.where(row_ids < half, len_ref[0], len_ref[1])
    for h in range(heads):
        qa[h * rows:(h + 1) * rows] = q_in[:, h * D:(h + 1) * D]
        g = g_in[:, h * D:(h + 1) * D]
        ga[h * rows:(h + 1) * rows] = jnp.where(live, g, jnp.zeros_like(g))

    def select(d, r, kv):
        u = 2 * d + r
        src, dst, own = z_block(d, r, kv), (xk, xv)[kv][u], (ka, va)[kv][u]
        own[0:BLOCK] = src[owners[0]]
        for j in X_ORDER:
            dst[j] = src[owners[j]]
            start([x_copy(d, r, kv, j)])

    def arrived(d, r, kv):
        wait_recv(x_copy(d, r, kv, j) for j in X_ORDER)

    def by_rows(size, body):
        def step(b, _):
            body(pl.ds(pl.multiple_of(b * size, size), size))
            return 0

        lax.fori_loop(0, total // size, step, 0)

    def own_fwd():
        mask = own_mask(len_ref, TRF, half, rows)
        rvt = rv[...].T

        def body(blk):
            t = jnp.where(mask, dot_nt(rk[...], qa[blk]) * (SCALE * LOG2E), -1e30)
            t_own[:, blk] = t
            m = jnp.max(t, axis=0, keepdims=True)
            e = jnp.exp2(t - m)
            m_s[:, blk] = m
            mo_s[:, blk] = m
            l_s[:, blk] = jnp.sum(e, axis=0, keepdims=True)
            ot[:, blk] = dot_nn(rvt, e.astype(BF16))

        by_rows(TRF, body)

    def turn_grads():
        for h in range(heads):
            at = slice(h * rows, (h + 1) * rows)
            gat[:, at] = ga[at].T

    def score(d, r):
        u = 2 * d + r
        arrived(d, r, 0)

        def body(blk):
            t = dot_nt(ka[u][...], qa[blk]) * (SCALE * LOG2E)
            ts[u][:, blk] = t
            m_s[:, blk] = jnp.maximum(m_s[:, blk], jnp.max(t, axis=0, keepdims=True))

        by_rows(TRF, body)

    def mix(d, r):
        u = 2 * d + r
        arrived(d, r, 1)
        vt[...] = va[u][...].T

        def body(blk):
            m = m_s[:, blk]
            e = jnp.exp2(ts[u][:, blk] - m)
            alpha = jnp.exp2(mo_s[:, blk] - m)
            mo_s[:, blk] = m
            l_s[:, blk] = l_s[:, blk] * alpha + jnp.sum(e, axis=0, keepdims=True)
            ot[:, blk] = ot[:, blk] * alpha + dot_nn(vt[...], e.astype(BF16))

        by_rows(TRF, body)

    def z_in(items):
        wait_recv(z_copy(*item) for item in items)

    wait_recv(t_copy(i, 0) for i in range(1, RANKS))
    start(z_copy(d, r, 0) for r in (0, 1) for d in (1, 3))
    select(0, 0, 0)
    select(0, 1, 0)
    wait_recv(t_copy(i, 1) for i in range(1, RANKS))
    select(0, 0, 1)
    select(0, 1, 1)
    own_fwd()
    score(0, 0)
    z_in([(1, 0, 0), (3, 0, 0)])
    start([z_copy(1, 0, 1), z_copy(3, 0, 1)])
    select(1, 0, 0)
    select(3, 0, 0)
    score(0, 1)
    mix(0, 0)
    z_in([(1, 1, 0), (3, 1, 0)])
    start([z_copy(1, 1, 1), z_copy(3, 1, 1)])
    select(1, 1, 0)
    select(3, 1, 0)
    mix(0, 1)
    turn_grads()
    score(1, 0)
    z_in([(1, 0, 1), (3, 0, 1)])
    start([z_copy(2, 0, 0), z_copy(2, 1, 0)])
    select(1, 0, 1)
    select(3, 0, 1)
    score(3, 0)
    score(1, 1)
    z_in([(1, 1, 1), (3, 1, 1)])
    start([z_copy(2, 0, 1), z_copy(2, 1, 1)])
    select(1, 1, 1)
    select(3, 1, 1)
    score(3, 1)
    mix(1, 0)
    z_in([(2, 0, 0), (2, 1, 0)])
    select(2, 0, 0)
    select(2, 1, 0)
    mix(3, 0)
    mix(1, 1)
    z_in([(2, 0, 1), (2, 1, 1)])
    select(2, 0, 1)
    select(2, 1, 1)
    mix(3, 1)
    score(2, 0)
    score(2, 1)
    mix(2, 0)
    mix(2, 1)

    def stats(blk):
        l = l_s[:, blk]
        o = ot[:, blk] / l
        ot[:, blk] = o
        d_s[:, blk] = jnp.sum(o * gat[:, blk].astype(F32), axis=0, keepdims=True)
        m_s[:, blk] = m_s[:, blk] + jnp.log2(l)
        dqt[:, blk] = jnp.zeros((D, TRF), F32)

    by_rows(TRF, stats)

    def write_out():
        for h in range(heads):
            o = ot[:, h * rows:(h + 1) * rows].T
            o_out[:, h * D:(h + 1) * D] = jnp.where(live, o, 0.0).astype(BF16)
        stores[0].start()

    def bwd_block(t, vs, kts, blk):
        qb, gb = qa[blk], ga[blk]
        p = jnp.exp2(t - m_s[:, blk])
        ds = (p * (dot_nt(vs, gb) - d_s[:, blk])).astype(BF16)
        dv = dot_nn(p.astype(BF16), gb)
        dk = dot_nn(ds, qb)
        dqt[:, blk] += dot_nn(kts, ds)
        return dk, dv

    def bwd(d, r):
        u = 2 * d + r
        kt[...] = ka[u][...].T
        acc_k[...] = jnp.zeros_like(acc_k)
        acc_v[...] = jnp.zeros_like(acc_v)

        def body(blk):
            dk, dv = bwd_block(ts[u][:, blk], va[u][...], kt[...], blk)
            acc_k[...] += dk
            acc_v[...] += dv

        by_rows(TRB, body)
        gu[u][:, 0] = (acc_k[...] * SCALE).astype(BF16).reshape(PEERS, BLOCK, D)
        gu[u][:, 1] = acc_v[...].astype(BF16).reshape(PEERS, BLOCK, D)
        start(gx_copy(d, r, j) for j in X_ORDER)

    def own_bwd():
        rkt = rk[...].T
        acc_k[:rows] = jnp.zeros((rows, D), F32)
        acc_v[:rows] = jnp.zeros((rows, D), F32)

        def body(blk):
            dk, dv = bwd_block(t_own[:, blk], rv[...], rkt, blk)
            acc_k[:rows] += dk
            acc_v[:rows] += dv

        by_rows(TRB, body)
        drk[...] = (acc_k[:rows] * SCALE).astype(BF16)
        drv[...] = acc_v[:rows].astype(BF16)
        for h in range(heads):
            dq_out[:, h * D:(h + 1) * D] = (dqt[:, h * rows:(h + 1) * rows] * SCALE).T.astype(BF16)
        for copy in stores[1:4]:
            copy.start()

    picks = [[(owners[j] == p).astype(F32) for j in range(PEERS)] for p in range(PROMPTS)]

    def reduce(d, r):
        u = 2 * d + r
        wait_recv(gx_copy(d, r, j) for j in X_ORDER)
        passing = (d, r) in ((1, 0), (3, 1))
        if passing:
            wait_recv([gz_copy(2, r)])

        def body(b, _):
            at = rows_of(b)
            for kv in range(2):
                terms = [gu[u][0, kv, at].astype(F32)] + [rgu[u][j, kv, at].astype(F32) for j in range(1, PEERS)]
                for p in range(PROMPTS):
                    value = terms[0] * picks[p][0]
                    for j in range(1, PEERS):
                        value = value + terms[j] * picks[p][j]
                    if passing:
                        value = value + relay[r][kv, p, at].astype(F32)
                    if d == 0:
                        own_sum[r][kv, p, at] = value
                    else:
                        su[u][kv, p, at] = value.astype(BF16)
            return 0

        lax.fori_loop(0, BLOCK // 16, body, 0)
        if d:
            start([gz_copy(d, r)])

    def finish(r):
        wait_recv(gz_copy(d, r) for d in (1, 3))

        def body(b, _):
            at = rows_of(b)
            for kv in range(2):
                for p in range(PROMPTS):
                    value = own_sum[r][kv, p, at]
                    for d in (1, 3):
                        value = value + rsu[2 * d + r][kv, p, at].astype(F32)
                    bo[r, kv, p, at] = value.astype(BF16)
            return 0

        lax.fori_loop(0, BLOCK // 16, body, 0)

    bwd(2, 0)
    bwd(2, 1)
    bwd(1, 1)
    reduce(2, 0)
    bwd(3, 0)
    reduce(2, 1)
    bwd(1, 0)
    write_out()
    reduce(1, 1)
    bwd(3, 1)
    reduce(3, 0)
    bwd(0, 0)
    reduce(1, 0)
    bwd(0, 1)
    reduce(3, 1)
    own_bwd()
    reduce(0, 0)
    finish(0)
    reduce(0, 1)
    finish(1)
    start(gt_copy(i) for i in range(1, RANKS))
    back[tensor] = bo[tensor // 4, :, :, rows_of(tensor % 4)]

    wait_send(t_copy(i, kv) for i, kv in t_all)
    wait_send(z_copy(d, r, kv) for d in range(1, Z) for r in range(2) for kv in range(2))
    wait_send(x_copy(d, r, kv, j) for d in range(Z) for r in range(2) for kv in range(2) for j in X_ORDER)
    wait_send(gx_copy(d, r, j) for d in range(Z) for r in range(2) for j in X_ORDER)
    wait_send(gz_copy(d, r) for d in range(1, Z) for r in range(2))

    wait_recv(gt_copy(i) for i in range(1, RANKS))
    for kv in range(2):
        for t in range(RANKS):
            for p in range(PROMPTS):
                at = p * RANKS * D + t * D
                (pk, pv)[kv][:, at:at + D] = back[t, kv, p]
        stores[4 + kv].start()
    wait_send(gt_copy(i) for i in range(1, RANKS))
    for copy in stores:
        copy.wait()


def attention(owner, lengths, pk, pv, q, g, rk, rv, comm=True):
    rows, width = q.shape
    total = rows * width // D
    hbm = pl.BlockSpec(memory_space=pl.ANY)
    sm = pl.BlockSpec(memory_space=pltpu.SMEM)
    vmem = pltpu.VMEM
    dma = pltpu.SemaphoreType.DMA
    units = Z * PARTS

    def some(count, shape, dtype=BF16):
        return [vmem(shape, dtype) for _ in range(count)]

    block = (PROMPTS, BLOCK, D)
    scratch = [
        vmem(pk.shape, BF16), vmem(pv.shape, BF16), vmem(q.shape, BF16), vmem(q.shape, BF16),
        vmem(rk.shape, BF16), vmem(rk.shape, BF16), vmem(q.shape, BF16), vmem(q.shape, BF16),
        vmem(rk.shape, BF16), vmem(rk.shape, BF16),
        vmem((RANKS, 2, PROMPTS, 16, D), BF16), vmem((RANKS, 2, PROMPTS, 16, D), BF16),
        vmem((PARTS, *block), BF16), vmem((PARTS, *block), BF16), some(units, block), some(units, block),
        some(units, (PEERS, BLOCK, D)), some(units, (PEERS, BLOCK, D)),
        some(units, (UNIT, D)), some(units, (UNIT, D)),
        some(units, (UNIT, total), F32), vmem((rows, total), F32),
        vmem((total, D), BF16), vmem((total, D), BF16), vmem((D, total), BF16),
        vmem((1, total), F32), vmem((1, total), F32), vmem((1, total), F32), vmem((1, total), F32),
        vmem((D, total), F32), vmem((D, total), F32), vmem((D, UNIT), BF16), vmem((D, UNIT), BF16),
        vmem((UNIT, D), F32), vmem((UNIT, D), F32),
        some(units, (PEERS, 2, BLOCK, D)), some(units, (PEERS, 2, BLOCK, D)),
        some(units, (2, *block)), some(units, (2, *block)), some(PARTS, (2, *block)),
        some(PARTS, (2, *block), F32), vmem((PARTS, 2, *block), BF16),
        dma((12,)), dma((2 * RANKS,)), dma((2 * RANKS,)), dma((2 * units,)), dma((2 * units,)),
        dma((2 * units * PEERS,)), dma((2 * units * PEERS,)), dma((units * PEERS,)), dma((units * PEERS,)),
        dma((units,)), dma((units,)), dma((RANKS,)), dma((RANKS,)),
    ]
    extra = dict(collective_id=0, has_side_effects=True) if comm else {}
    return pl.pallas_call(
        functools.partial(kernel, comm),
        out_shape=(
            jax.ShapeDtypeStruct(q.shape, BF16),
            jax.ShapeDtypeStruct(q.shape, BF16),
            jax.ShapeDtypeStruct(rk.shape, BF16),
            jax.ShapeDtypeStruct(rk.shape, BF16),
            jax.ShapeDtypeStruct(pk.shape, BF16),
            jax.ShapeDtypeStruct(pv.shape, BF16),
        ),
        in_specs=[sm, sm] + [hbm] * 6,
        out_specs=(hbm,) * 6,
        scratch_shapes=scratch,
        compiler_params=pltpu.CompilerParams(vmem_limit_bytes=62 * 2 ** 20, **extra),
    )(owner, lengths, pk, pv, q, g, rk, rv)


def local(q, rk, rv, prompt_keys, prompt_values, g, lengths, prompt_of):
    shape = prompt_keys.shape
    flat = (shape[0], shape[1] * shape[2])
    o, dq, drk, drv, dpk, dpv = attention(
        prompt_of, lengths, prompt_keys.reshape(flat), prompt_values.reshape(flat), q, g, rk, rv
    )
    return o, dq, drk, drv, dpk.reshape(shape), dpv.reshape(shape)


def solution(mesh):
    heads = P("dp", "tensor")
    prompt = P(("dp", "tensor"), None, None)
    return jax.shard_map(
        local,
        mesh=mesh,
        in_specs=(heads, heads, heads, prompt, prompt, heads, P("dp"), P()),
        out_specs=(heads, heads, heads, heads, prompt, prompt),
        check_vma=False,
    )
```

time: 120 us -> 94.9 us (0.79)
  Pallas kernels: 110 us -> 84.6 us
    pallas_call x1, Pallas kernels: 110 us -> 84.6 us  [attention(): pl.pallas_call(functools.partial(kernel, comm), out_shape=(jax.ShapeDtype...]
    reshape x0 -> x2, local copies, waits for them, and re-layouts: none -> 3.32 us  [local(): return (o, dq, drk, drv, dpk.reshape(shape), dpv.reshape(shape))]
    unnamed x18 -> x16, local copies, waits for them, and re-layouts: 5.99 us -> 5.93 us
where the time goes in v3:
time: 94.9 us; the launch traced here: 94.6 us
  Pallas kernels  84.6 us (89%)
  local copies, waits for them, and re-layouts  9.25 us (10%)
    pallas_call x1, Pallas kernels, attention(): pl.pallas_call(functools.partial(kernel, comm), out_shape=(jax.ShapeDtype...  84.6 us
    unnamed x16, local copies, waits for them, and re-layouts  5.93 us
    reshape x2, local copies, waits for them, and re-layouts, local(): return (o, dq, drk, drv, dpk.reshape(shape), dpv.reshape(shape))  3.32 us

profile of v3, /device:TPU:1, one launch (start us, length us, event | category | flops | bytes accessed | tf_op | source)
XLA Modules:
  0.0 94.6 jit_solution(2493208990434464183)
XLA Ops:
  0.6 0.0 copy-start.2
  0.6 1.6 %copy.14 = bf16[2,8,4,1024]{3,1,2,0:T(8,128)(2,1)} copy(bf16[2,8,4,1024]{3,2,1,0:T(4,128)(2,1)} %bitcast.6) | data formatting | bytes 262144
  2.3 0.0 copy-done.2
  2.3 0.7 copy.15
  3.0 84.6 %shard_map.127 = (bf16[256,1024]{1,0:T(8,128)(2,1)}, bf16[256,1024]{1,0:T(8,128)(2,1)}, bf16[256,128]{1,0:T(8,128)(2,1)}, bf16[256,128]{1,0:T(8,128)(2,1)}, bf16...) custom-call(s32[32]{0:T(128)} %owner_ref.1, s32[2]{0:T(128)} %len_ref.1, bf16[16,4096]{1,0:T(8,128)(2,1)} %bitcast.4, ...), custom_call_target="tpu_custom_call" | custom-call | tf_op jit(solution)/shard_map/pallas_call | solution.py:466
  87.6 0.0 copy-start.1
  87.6 1.7 %reshape.26 = bf16[16,4,1024]{2,1,0:T(4,128)(2,1)} reshape(bf16[16,4096]{1,0:T(8,128)(2,1)} %get-tuple-element.16) | data formatting | bytes 262144 | tf_op jit(solution)/shard_map/reshape | solution.py:489
  89.3 1.6 %reshape.27 = bf16[16,4,1024]{2,1,0:T(4,128)(2,1)} reshape(bf16[16,4096]{1,0:T(8,128)(2,1)} %get-tuple-element.17) | data formatting | bytes 262144 | tf_op jit(solution)/shard_map/reshape | solution.py:489
  91.0 0.0 copy-done.1
  91.0 0.0 copy-start
  91.0 0.8 copy.20
  91.8 0.4 copy-done
  92.2 0.0 copy-start.4
  92.2 0.8 copy.21
  93.0 0.1 copy-done.4
  93.1 0.0 copy-start.3
  93.1 0.6 copy.22
  93.7 0.2 copy-done.3
  93.9 0.6 copy.23
Async XLA Ops:
  0.6 1.6 %copy-start.2 = (bf16[16,4,1024]{2,1,0:T(4,128)(2,1)S(1)}, bf16[16,4,1024]{2,1,0:T(4,128)(2,1)}, u32[]{:S(2)}) copy-start(bf16[16,4,1024]{2,1,0:T(4,128)(2,1)} %param.12) | copy-start | bytes 393220
  87.6 3.3 %copy-start.1 = (bf16[256,1024]{1,0:T(8,128)(2,1)S(1)}, bf16[256,1024]{1,0:T(8,128)(2,1)}, u32[]{:S(2)}) copy-start(bf16[256,1024]{1,0:T(8,128)(2,1)} %get-tuple-element.24) | copy-start | bytes 1572868
  91.0 1.2 %copy-start = (bf16[256,1024]{1,0:T(8,128)(2,1)S(1)}, bf16[256,1024]{1,0:T(8,128)(2,1)}, u32[]{:S(2)}) copy-start(bf16[256,1024]{1,0:T(8,128)(2,1)} %get-tuple-element.25) | copy-start | bytes 1572868
  92.2 0.9 copy-start.4
  93.1 0.9 copy-start.3

commit v4 on v3

--- a/solution.py
+++ b/solution.py
@@ -20,8 +20,8 @@
 PARTS = 2
 BLOCK = 64
 UNIT = PEERS * BLOCK
-TRF, TRB = 1024, 1024
-X_ORDER = (2, 6, 3, 7, 4, 5, 1)
+TRF, TRB = 1024, 2048
+X_ORDER = (4, 5, 2, 6, 3, 7, 1)
 
 
 def dot_nt(a, b):
@@ -110,10 +110,11 @@
         step = {1: -1, 3: 1, 2: (-1, 1)[r]}[d]
         return remote(su[u], dst, gz_send.at[u], gz_recv.at[u], (z_peer(step), tensor))
 
-    def gt_copy(i):
-        to = t_peer(i)
-        return remote(bo.at[to // 4, :, :, rows_of(to % 4)], back.at[tensor],
-                      gt_send.at[i], gt_recv.at[i], (dp, to))
+    def gt_copy(r, k):
+        to_y = (y_at + k) % 4
+        at = (r + 2 - zl_at) % 2 * 4 + k
+        return remote(bo.at[r, :, :, rows_of(to_y)], back.at[tensor],
+                      gt_send.at[at], gt_recv.at[at], (dp, r * 4 + to_y))
 
     def start(copies):
         if comm:
@@ -146,17 +147,14 @@
         for i in range(1, RANKS):
             pl.semaphore_signal(barrier, inc=1, device_id=(dp, t_back(i)), device_id_type=MESH)
 
+    t_all = [(i, kv) for kv in range(2) for i in range(1, RANKS)]
     for kv in range(2):
         loads[kv].wait()
         for t in range(RANKS):
-            for p in range(PROMPTS):
-                at = p * RANKS * D + t * D
-                pin[t, kv, p] = (pk, pv)[kv][:, at:at + D]
-    if comm:
-        pl.semaphore_wait(barrier, PEERS - 1 + 2 + RANKS - 1)
-
-    t_all = [(i, kv) for kv in range(2) for i in range(1, RANKS)]
-    start(t_copy(i, kv) for i, kv in t_all)
+            pin[t, kv] = jnp.swapaxes((pk, pv)[kv][:, :, t * D:(t + 1) * D], 0, 1)
+        if comm and kv == 0:
+            pl.semaphore_wait(barrier, PEERS - 1 + 2 + RANKS - 1)
+        start(t_copy(i, kv) for i in range(1, RANKS))
     for kv in range(2):
         (own_zk, own_zv)[kv][tensor // 4, :, rows_of(tensor % 4)] = pin[tensor, kv]
     for copy in loads[2:]:
@@ -310,21 +308,25 @@
         dqt[:, blk] += dot_nn(kts, ds)
         return dk, dv
 
-    def bwd(d, r):
+    def bwd(d, r, cuts=1):
         u = 2 * d + r
         kt[...] = ka[u][...].T
-        acc_k[...] = jnp.zeros_like(acc_k)
-        acc_v[...] = jnp.zeros_like(acc_v)
-
-        def body(blk):
-            dk, dv = bwd_block(ts[u][:, blk], va[u][...], kt[...], blk)
-            acc_k[...] += dk
-            acc_v[...] += dv
-
-        by_rows(TRB, body)
-        gu[u][:, 0] = (acc_k[...] * SCALE).astype(BF16).reshape(PEERS, BLOCK, D)
-        gu[u][:, 1] = acc_v[...].astype(BF16).reshape(PEERS, BLOCK, D)
-        start(gx_copy(d, r, j) for j in X_ORDER)
+        for cut in range(cuts):
+            peers = PEERS // cuts
+            mine = slice(cut * peers, (cut + 1) * peers)
+            keys = slice(cut * peers * BLOCK, (cut + 1) * peers * BLOCK)
+            acc_k[keys] = jnp.zeros((peers * BLOCK, D), F32)
+            acc_v[keys] = jnp.zeros((peers * BLOCK, D), F32)
+
+            def body(blk):
+                dk, dv = bwd_block(ts[u][keys, blk], va[u][keys], kt[:, keys], blk)
+                acc_k[keys] += dk
+                acc_v[keys] += dv
+
+            by_rows(TRB, body)
+            gu[u][mine, 0] = (acc_k[keys] * SCALE).astype(BF16).reshape(peers, BLOCK, D)
+            gu[u][mine, 1] = acc_v[keys].astype(BF16).reshape(peers, BLOCK, D)
+            start(gx_copy(d, r, j) for j in X_ORDER if j // peers == cut)
 
     def own_bwd():
         rkt = rk[...].T
@@ -387,8 +389,12 @@
             return 0
 
         lax.fori_loop(0, BLOCK // 16, body, 0)
-
-    bwd(2, 0)
+        if comm:
+            for k in range(1, 4):
+                gt_copy(r, k).start()
+            pl.when(zl_at != r)(gt_copy(r, 0).start)
+
+    bwd(2, 0, 2)
     bwd(2, 1)
     bwd(1, 1)
     reduce(2, 0)
@@ -408,7 +414,6 @@
     finish(0)
     reduce(0, 1)
     finish(1)
-    start(gt_copy(i) for i in range(1, RANKS))
     back[tensor] = bo[tensor // 4, :, :, rows_of(tensor % 4)]
 
     wait_send(t_copy(i, kv) for i, kv in t_all)
@@ -417,14 +422,14 @@
     wait_send(gx_copy(d, r, j) for d in range(Z) for r in range(2) for j in X_ORDER)
     wait_send(gz_copy(d, r) for d in range(1, Z) for r in range(2))
 
-    wait_recv(gt_copy(i) for i in range(1, RANKS))
+    gt_all = [remote(bo.at[0, :, :, rows_of(0)], back.at[0], gt_send.at[i], gt_recv.at[i], (dp, t_peer(i)))
+              for i in range(1, RANKS)]
+    wait_recv(gt_all)
     for kv in range(2):
         for t in range(RANKS):
-            for p in range(PROMPTS):
-                at = p * RANKS * D + t * D
-                (pk, pv)[kv][:, at:at + D] = back[t, kv, p]
+            (pk, pv)[kv][:, :, t * D:(t + 1) * D] = jnp.swapaxes(back[t, kv], 0, 1)
         stores[4 + kv].start()
-    wait_send(gt_copy(i) for i in range(1, RANKS))
+    wait_send(gt_all)
     for copy in stores:
         copy.wait()
 
@@ -480,13 +485,40 @@
     )(owner, lengths, pk, pv, q, g, rk, rv)
 
 
+def settle_kernel(*refs):
+    count = len(refs) // 3
+    given, wanted, held = refs[:count], refs[count:2 * count], refs[2 * count:3 * count]
+    sems = refs[-1]
+    pieces = [(n, slice(at, at + held[n].shape[0] // 2))
+              for n in range(count) for at in (0, held[n].shape[0] // 2)]
+    loads = [pltpu.make_async_copy(given[n].at[at], held[n].at[at], sems.at[0, i])
+             for i, (n, at) in enumerate(pieces)]
+    stores = [pltpu.make_async_copy(held[n].at[at], wanted[n].at[at], sems.at[1, i])
+              for i, (n, at) in enumerate(pieces)]
+    for load in loads:
+        load.start()
+    for load, store in zip(loads, stores):
+        load.wait()
+        store.start()
+    for store in stores:
+        store.wait()
+
+
+def settle(*arrays):
+    hbm = pl.BlockSpec(memory_space=pl.ANY)
+    return pl.pallas_call(
+        settle_kernel,
+        out_shape=tuple(jax.ShapeDtypeStruct(a.shape, a.dtype) for a in arrays),
+        in_specs=[hbm] * len(arrays),
+        out_specs=(hbm,) * len(arrays),
+        scratch_shapes=[pltpu.VMEM(a.shape, a.dtype) for a in arrays]
+        + [pltpu.SemaphoreType.DMA((2, 2 * len(arrays)))],
+        compiler_params=pltpu.CompilerParams(vmem_limit_bytes=60 * 2 ** 20),
+    )(*arrays)
+
+
 def local(q, rk, rv, prompt_keys, prompt_values, g, lengths, prompt_of):
-    shape = prompt_keys.shape
-    flat = (shape[0], shape[1] * shape[2])
-    o, dq, drk, drv, dpk, dpv = attention(
-        prompt_of, lengths, prompt_keys.reshape(flat), prompt_values.reshape(flat), q, g, rk, rv
-    )
-    return o, dq, drk, drv, dpk.reshape(shape), dpv.reshape(shape)
+    return settle(*attention(prompt_of, lengths, prompt_keys, prompt_values, q, g, rk, rv))
 
 
 def solution(mesh):

time: 94.9 us -> 85.9 us (0.905)
  the two profiles are of different devices: /device:TPU:1 before, /device:TPU:32 now
where the time goes in v4:
time: 85.9 us; the launch traced here: 85.8 us
  Pallas kernels  85 us (99%)
    pallas_call x1, Pallas kernels, attention(): pl.pallas_call(functools.partial(kernel, comm), out_shape=(jax.ShapeDtype...  82.7 us
    pallas_call x1, Pallas kernels, settle(): pl.pallas_call(settle_kernel, out_shape=tuple((jax.ShapeDtypeStruct(a.sha...  2.24 us

profile of v4, /device:TPU:32, one launch (start us, length us, event | category | flops | bytes accessed | tf_op | source)
XLA Modules:
  0.0 85.8 jit_solution(15440514828761984325)
XLA Ops:
  0.6 82.7 %shard_map.127 = (bf16[256,1024]{1,0:T(8,128)(2,1)}, bf16[256,1024]{1,0:T(8,128)(2,1)}, bf16[256,128]{1,0:T(8,128)(2,1)}, bf16[256,128]{1,0:T(8,128)(2,1)}, bf16...) custom-call(s32[32]{0:T(128)} %owner_ref.1, s32[2]{0:T(128)} %len_ref.1, bf16[16,4,1024]{2,1,0:T(4,128)(2,1)} %pk_hbm.1, ...), custom_call_target="tpu_custom_call" | custom-call | tf_op jit(solution)/shard_map/pallas_call | solution.py:471
  83.4 2.2 %shard_map.128 = (bf16[256,1024]{1,0:T(8,128)(2,1)}, bf16[256,1024]{1,0:T(8,128)(2,1)}, bf16[256,128]{1,0:T(8,128)(2,1)}, bf16[256,128]{1,0:T(8,128)(2,1)}, bf16...) custom-call(bf16[256,1024]{1,0:T(8,128)(2,1)} %get-tuple-element.12.refs_0_, ...), custom_call_target="tpu_custom_call" | custom-call | tf_op jit(solution)/shard_map/pallas_call | solution.py:509
